TPU v7x, 128 devices: a whole 4x4x4 slice. The times are simulated.
128 devices in a mesh: mem: 8 (over y, x_lo), seq: 16 (over z, x_hi, core).
Axes of the slice: x: 4 (x_hi: 2, x_lo: 2; x = x_hi * 2 + x_lo), y: 4, z: 4, core: 2. Of those that a mesh axis runs over, the one named last changes fastest.
Arguments:
- state_field: bfloat16 [64, 2048, 512], P('mem', 'seq'), may hold values from -6 to 6
- gain_space: float32 [512], replicated, may hold values from 0.25 to 1.75
- w_qkv_space: bfloat16 [512, 1536], replicated, may hold values from -0.2788369 to 0.2788369
- w_out_space: bfloat16 [512, 512], replicated, may hold values from -0.25 to 0.25
- gain_member: float32 [512], replicated, may hold values from 0.25 to 1.75
- w_qkv_member: bfloat16 [512, 1536], replicated, may hold values from -0.28079004 to 0.28079004
- w_out_member: bfloat16 [512, 512], replicated, may hold values from -0.25 to 0.25
- gain_mlp: float32 [512], replicated, may hold values from 0.25 to 1.75
- w_up: bfloat16 [512, 2048], replicated, may hold values from -0.25 to 0.25
- w_down: bfloat16 [2048, 512], replicated, may hold values from -0.125 to 0.125
Outputs:
- corrected: bfloat16 [64, 2048, 512], P('mem', 'seq')
All inputs are finite; a program needn't handle non-finite values.
Results may differ from a plain program's by a relative error of at most 0.018.
Values may be sent and summed in bfloat16 or wider, within the bound.
No kernel may reach another device: no remote copies, remote signals or barrier semaphores. Data moves between devices by JAX's collectives and lax.ppermute only.
A program may use at most 256 MiB of HBM per device.

v0:
```python
import jax
import jax.numpy as jnp
from jax import lax
from jax.sharding import PartitionSpec as P

HEADS = 8


def normed(values, gain):
    floats = values.astype(jnp.float32)
    scaled = floats * lax.rsqrt(jnp.mean(floats * floats, axis=-1, keepdims=True) + 1e-05)
    return (scaled * gain).astype(jnp.bfloat16)


def project(values, weight):
    rows = values.reshape(-1, values.shape[-1])
    return jnp.dot(rows, weight, preferred_element_type=jnp.float32).reshape(
        values.shape[:-1] + (weight.shape[1],)
    )


def space_single(pair_rows):
    head_dim = pair_rows.shape[-1] // 3
    queries = pair_rows[:, :head_dim]
    keys_here = pair_rows[:, head_dim : 2 * head_dim]
    values = pair_rows[:, 2 * head_dim :]
    scores = jnp.einsum(
        "qc,kc->qk", queries, keys_here, preferred_element_type=jnp.float32
    ) * head_dim ** (-0.5)
    peaks = jnp.max(scores, axis=-1, keepdims=True)
    weights = jnp.exp(scores - peaks)
    totals = jnp.sum(weights, axis=-1, keepdims=True)
    mixed = (
        jnp.dot(weights.astype(jnp.bfloat16), values, preferred_element_type=jnp.float32) / totals
    )
    return mixed.astype(jnp.bfloat16)


def member_attend(queries, key_value):
    model_width = queries.shape[-1]
    head_dim = model_width // HEADS
    count, tokens_here = (queries.shape[0], queries.shape[1])
    others = key_value.shape[0]
    q = queries.reshape(count, tokens_here, HEADS, head_dim)
    k = key_value[..., :model_width].reshape(others, tokens_here, HEADS, head_dim)
    v = key_value[..., model_width:].reshape(others, tokens_here, HEADS, head_dim)
    scores = jnp.einsum("mthc,nthc->thmn", q, k, preferred_element_type=jnp.float32) * head_dim ** (
        -0.5
    )
    peaks = jnp.max(scores, axis=-1, keepdims=True)
    weights = jnp.exp(scores - peaks)
    totals = jnp.sum(weights, axis=-1)
    mixed = jnp.einsum(
        "thmn,nthc->mthc", weights.astype(jnp.bfloat16), v, preferred_element_type=jnp.float32
    )
    mixed = mixed / jnp.transpose(totals, (2, 0, 1))[..., None]
    return mixed.reshape(count, tokens_here, model_width).astype(jnp.bfloat16)


def per_device(
    state_field,
    gain_space,
    w_qkv_space,
    w_out_space,
    gain_member,
    w_qkv_member,
    w_out_member,
    gain_mlp,
    w_up,
    w_down,
):
    mem_dev, tok_dev, model_width = state_field.shape
    head_dim = model_width // HEADS
    normed_space = normed(state_field, gain_space)
    head_weight = (
        w_qkv_space.reshape(model_width, 3, HEADS, head_dim)
        .transpose(0, 2, 1, 3)
        .reshape(model_width, HEADS, 3 * head_dim)
    )
    packed = jnp.einsum(
        "mtd,dhc->mhtc", normed_space, head_weight, preferred_element_type=jnp.float32
    ).astype(jnp.bfloat16)
    seq_groups = lax.axis_size("seq")
    pair_count = mem_dev * HEADS
    grouped_pairs = packed.reshape(seq_groups, pair_count // seq_groups, tok_dev, 3 * head_dim)
    inner = lax.map(
        space_single,
        lax.all_to_all(grouped_pairs, "seq", split_axis=0, concat_axis=2, tiled=True)[0],
    )
    pair_out = inner[None]
    returned = lax.all_to_all(pair_out, "seq", split_axis=2, concat_axis=0, tiled=True)
    mixed = returned.reshape(mem_dev, HEADS, tok_dev, head_dim)
    attended = jnp.einsum(
        "mhtc,hcd->mtd",
        mixed,
        w_out_space.reshape(HEADS, head_dim, model_width),
        preferred_element_type=jnp.float32,
    )
    after_space = (state_field.astype(jnp.float32) + attended).astype(jnp.bfloat16)
    qkv_member = project(normed(after_space, gain_member), w_qkv_member).astype(jnp.bfloat16)
    key_value = lax.all_gather(qkv_member[..., model_width:], "mem", axis=0, tiled=True)
    member_mix = member_attend(qkv_member[..., :model_width], key_value)
    after_member = (after_space.astype(jnp.float32) + project(member_mix, w_out_member)).astype(
        jnp.bfloat16
    )
    hidden = jax.nn.gelu(project(normed(after_member, gain_mlp), w_up), approximate=True).astype(
        jnp.bfloat16
    )
    return (after_member.astype(jnp.float32) + project(hidden, w_down)).astype(jnp.bfloat16)


def solution(mesh):
    in_specs = (P("mem", "seq", None), P(), P(), P(), P(), P(), P(), P(), P(), P())
    out_specs = P("mem", "seq", None)
    return jax.shard_map(
        per_device, mesh=mesh, in_specs=in_specs, out_specs=out_specs, check_vma=False
    )
```

profile of v0, /device:TPU:0, one launch (start us, length us, event | category | flops | bytes accessed | tf_op | source)
XLA Modules:
  0.0 674.8 jit_solution(7150895203774502719)
XLA Ops:
  6.5 1.6 fusion.34
  8.2 2.6 copy.40
  10.8 1.5 copy.41
  12.4 3.5 convolution_convert_fusion.1
  15.9 8.0 %all-to-all-start = ((bf16[16,4,128,192]{2,3,1,0:T(8,128)(2,1)}), bf16[16,4,128,192]{2,3,1,0:T(8,128)(2,1)}, u32[]{:S(2)}, u32[]{:S(2)}) async-start(bf16[16,4,128,192]{2,3,1,0:T(8,128)(2,1)} %bitcast.84), calls=%async_computation | async-start | bytes 6291456 | tf_op jit(solution)/shard_map/all_to_all | solution.py:88
  24.0 40.6 %all-to-all-done = bf16[16,4,128,192]{2,3,1,0:T(8,128)(2,1)} async-done(((bf16[16,4,128,192]{2,3,1,0:T(8,128)(2,1)}), bf16[16,4,128,192]{2,3,1,0:T(8,128)(2,1)}, u32[]{:S(2)}, u32[]{:S(2)}) %all-to-all-start) | async-done | bytes 3145760 | tf_op jit(solution)/shard_map/all_to_all | solution.py:88
  64.5 6.0 copy.42
  70.5 101.6 %while.10 = (s32[]{:T(128)}, bf16[4,2048,64]{1,2,0:T(8,128)(2,1)S(1)}, bf16[4,2048,192]{2,1,0:T(8,128)(2,1)}, s32[]{:T(128)}) while((s32[]{:T(128)}, bf16[4,2048,64]{1,2,0:T(8,128)(2,1)S(1)}, bf16[4,2048,192]{2,1,0:T(8,128)(2,1)}, s32[]{:T(128)}) %tuple.30), condition=%wide.region_4.5_spmd, body=%wide.region_1.4_spmd.sunk | while | flops 1107554304 | bytes 53518404 | solution.py:86
  71.8 8.1 %multiply_reduce_fusion.3 = (f32[2048]{0:T(1024)S(1)}, f32[2048,2048]{0,1:T(8,128)}) fusion(bf16[2048,192]{1,0:T(8,128)(2,1)S(1)} %dynamic-slice_bitcast_fusion.2), kind=kOutput, calls=%fused_computation.1.clone.1 | convolution fusion | flops 545257472 | bytes 17571840 | tf_op jit(solution)/shard_map/while/body/eval_jaxpr/qc,kc->qk/dot_general | solution.py:27
  79.9 8.6 %fusion.94 = f32[2048]{0:T(1024)S(1)} fusion(f32[2048,2048]{0,1:T(8,128)} %get-tuple-element.60, f32[2048]{0:T(1024)S(1)} %get-tuple-element.61), kind=kLoop, calls=%fused_computation.2.clone.1 | loop fusion | flops 12580864 | bytes 16793600 | tf_op jit(solution)/shard_map/while/body/eval_jaxpr/reduce_sum | solution.py:32
  88.5 7.4 %fusion.95 = bf16[4,2048,64]{1,2,0:T(8,128)(2,1)S(1)} fusion(bf16[4,2048,64]{1,2,0:T(8,128)(2,1)S(1)} %get-tuple-element.67, s32[]{:T(128)S(6)} %copy.61, f32[2048,2048]{0,1:T(8,128)} %get-tuple-element.60, f32[2048]{0:T(1024)S(1)} %get-tuple-element.61, bf16[2048,192]{1,0:T(8,128)(2,1)S(1)} %dynamic-slice_bitcast_fusion.2, f32[2048]{0:T(1024)S(1)} %fusion.94), kind=kOutput, calls=%fused_computation.8.clone.1 | convolution fusion | flops 549715968 | bytes 17580036 | tf_op jit(solution)/shard_map/while/body/eval_jaxpr/dot_general | solution.py:34
  95.9 1.3 dynamic-slice_bitcast_fusion.2
  97.2 8.1 %multiply_reduce_fusion.3 = (f32[2048]{0:T(1024)S(1)}, f32[2048,2048]{0,1:T(8,128)}) fusion(bf16[2048,192]{1,0:T(8,128)(2,1)S(1)} %dynamic-slice_bitcast_fusion.2), kind=kOutput, calls=%fused_computation.1.clone.1 | convolution fusion | flops 545257472 | bytes 17571840 | tf_op jit(solution)/shard_map/while/body/eval_jaxpr/qc,kc->qk/dot_general | solution.py:27
  105.3 8.6 %fusion.94 = f32[2048]{0:T(1024)S(1)} fusion(f32[2048,2048]{0,1:T(8,128)} %get-tuple-element.60, f32[2048]{0:T(1024)S(1)} %get-tuple-element.61), kind=kLoop, calls=%fused_computation.2.clone.1 | loop fusion | flops 12580864 | bytes 16793600 | tf_op jit(solution)/shard_map/while/body/eval_jaxpr/reduce_sum | solution.py:32
  113.9 7.4 %fusion.95 = bf16[4,2048,64]{1,2,0:T(8,128)(2,1)S(1)} fusion(bf16[4,2048,64]{1,2,0:T(8,128)(2,1)S(1)} %get-tuple-element.67, s32[]{:T(128)S(6)} %copy.61, f32[2048,2048]{0,1:T(8,128)} %get-tuple-element.60, f32[2048]{0:T(1024)S(1)} %get-tuple-element.61, bf16[2048,192]{1,0:T(8,128)(2,1)S(1)} %dynamic-slice_bitcast_fusion.2, f32[2048]{0:T(1024)S(1)} %fusion.94), kind=kOutput, calls=%fused_computation.8.clone.1 | convolution fusion | flops 549715968 | bytes 17580036 | tf_op jit(solution)/shard_map/while/body/eval_jaxpr/dot_general | solution.py:34
  121.3 1.3 dynamic-slice_bitcast_fusion.2
  122.6 8.1 %multiply_reduce_fusion.3 = (f32[2048]{0:T(1024)S(1)}, f32[2048,2048]{0,1:T(8,128)}) fusion(bf16[2048,192]{1,0:T(8,128)(2,1)S(1)} %dynamic-slice_bitcast_fusion.2), kind=kOutput, calls=%fused_computation.1.clone.1 | convolution fusion | flops 545257472 | bytes 17571840 | tf_op jit(solution)/shard_map/while/body/eval_jaxpr/qc,kc->qk/dot_general | solution.py:27
  130.7 8.6 %fusion.94 = f32[2048]{0:T(1024)S(1)} fusion(f32[2048,2048]{0,1:T(8,128)} %get-tuple-element.60, f32[2048]{0:T(1024)S(1)} %get-tuple-element.61), kind=kLoop, calls=%fused_computation.2.clone.1 | loop fusion | flops 12580864 | bytes 16793600 | tf_op jit(solution)/shard_map/while/body/eval_jaxpr/reduce_sum | solution.py:32
  139.3 7.4 %fusion.95 = bf16[4,2048,64]{1,2,0:T(8,128)(2,1)S(1)} fusion(bf16[4,2048,64]{1,2,0:T(8,128)(2,1)S(1)} %get-tuple-element.67, s32[]{:T(128)S(6)} %copy.61, f32[2048,2048]{0,1:T(8,128)} %get-tuple-element.60, f32[2048]{0:T(1024)S(1)} %get-tuple-element.61, bf16[2048,192]{1,0:T(8,128)(2,1)S(1)} %dynamic-slice_bitcast_fusion.2, f32[2048]{0:T(1024)S(1)} %fusion.94), kind=kOutput, calls=%fused_computation.8.clone.1 | convolution fusion | flops 549715968 | bytes 17580036 | tf_op jit(solution)/shard_map/while/body/eval_jaxpr/dot_general | solution.py:34
  146.7 1.3 dynamic-slice_bitcast_fusion.2
  148.0 8.1 %multiply_reduce_fusion.3 = (f32[2048]{0:T(1024)S(1)}, f32[2048,2048]{0,1:T(8,128)}) fusion(bf16[2048,192]{1,0:T(8,128)(2,1)S(1)} %dynamic-slice_bitcast_fusion.2), kind=kOutput, calls=%fused_computation.1.clone.1 | convolution fusion | flops 545257472 | bytes 17571840 | tf_op jit(solution)/shard_map/while/body/eval_jaxpr/qc,kc->qk/dot_general | solution.py:27
  156.1 8.6 %fusion.94 = f32[2048]{0:T(1024)S(1)} fusion(f32[2048,2048]{0,1:T(8,128)} %get-tuple-element.60, f32[2048]{0:T(1024)S(1)} %get-tuple-element.61), kind=kLoop, calls=%fused_computation.2.clone.1 | loop fusion | flops 12580864 | bytes 16793600 | tf_op jit(solution)/shard_map/while/body/eval_jaxpr/reduce_sum | solution.py:32
  164.7 7.4 %fusion.95 = bf16[4,2048,64]{1,2,0:T(8,128)(2,1)S(1)} fusion(bf16[4,2048,64]{1,2,0:T(8,128)(2,1)S(1)} %get-tuple-element.67, s32[]{:T(128)S(6)} %copy.61, f32[2048,2048]{0,1:T(8,128)} %get-tuple-element.60, f32[2048]{0:T(1024)S(1)} %get-tuple-element.61, bf16[2048,192]{1,0:T(8,128)(2,1)S(1)} %dynamic-slice_bitcast_fusion.2, f32[2048]{0:T(1024)S(1)} %fusion.94), kind=kOutput, calls=%fused_computation.8.clone.1 | convolution fusion | flops 549715968 | bytes 17580036 | tf_op jit(solution)/shard_map/while/body/eval_jaxpr/dot_general | solution.py:34
  172.1 2.5 copy.43
  174.7 3.0 bitcast_bitcast_fusion
  177.6 4.4 reshape.92
  182.0 21.3 %all_to_all.30 = bf16[16,2,16384]{2,1,0:T(2,128)(2,1)} all-to-all(bf16[16,2,16384]{2,1,0:T(2,128)(2,1)S(1)} %reshape.92), channel_id=1, replica_groups=mesh['mem'=8,'seq'=16] {'seq'}, dimensions={0} | all-to-all | bytes 2097152 | tf_op jit(solution)/shard_map/all_to_all | solution.py:91
  203.3 5.3 reshape.93
  208.6 2.8 copy.44
  211.4 2.3 fusion.38
  213.7 3.6 convolution_convert_fusion
  217.3 1.7 copy-done.1
  219.0 1.6 slice.28
  220.7 2.3 slice.30
  222.9 1.6 copy.46
  224.5 3.8 copy.48
  228.3 315.0 %all-gather.2.cloned.1.call-done = bf16[64,128,1024]{2,1,0:T(8,128)(2,1)} async-done(((bf16[8,128,1024]{2,1,0:T(8,128)(2,1)}), bf16[64,128,1024]{2,1,0:T(8,128)(2,1)}) %all-gather.2.cloned.1.call-update) | async-done | bytes 16777232 | tf_op jit(solution)/shard_map/all_gather | solution.py:101
  543.3 11.6 %fusion.80 = (bf16[64,128,512]{2,1,0:T(8,128)(2,1)}, bf16[64,128,512]{2,1,0:T(8,128)(2,1)}) fusion(bf16[64,128,1024]{2,1,0:T(8,128)(2,1)} %all-gather.2.cloned.1.call-done), kind=kLoop, calls=%fused_computation.76 | loop fusion | bytes 33554432 | tf_op jit(solution)/shard_map/slice | solution.py:45
  554.9 11.9 %copy.57 = bf16[64,128,512]{1,2,0:T(8,128)(2,1)} copy(bf16[64,128,512]{2,1,0:T(8,128)(2,1)} %get-tuple-element.31) | data formatting | bytes 16777216
  566.8 24.0 %copy.49 = bf16[64,128,8,64]{3,0,2,1:T(8,128)(2,1)} copy(bf16[64,128,8,64]{1,3,2,0:T(8,128)(2,1)} %bitcast.78) | data formatting | bytes 16777216 | tf_op jit(solution)/shard_map/reshape | solution.py:45
  590.8 11.9 %copy.56 = bf16[64,128,512]{1,2,0:T(8,128)(2,1)} copy(bf16[64,128,512]{2,1,0:T(8,128)(2,1)} %get-tuple-element.32) | data formatting | bytes 16777216
  602.7 24.0 %copy.50 = bf16[64,128,8,64]{3,0,2,1:T(8,128)(2,1)} copy(bf16[64,128,8,64]{1,3,2,0:T(8,128)(2,1)} %bitcast.79) | data formatting | bytes 16777216 | tf_op jit(solution)/shard_map/reshape | solution.py:46
  626.7 12.8 %multiply_reduce_fusion.1 = (f32[128,8,8]{2,1,0:T(8,128)S(1)}, f32[128,8,8,64]{3,2,1,0:T(8,128)S(1)}) fusion(bf16[8,128,8,64]{3,0,2,1:T(8,128)(2,1)} %copy.48, bf16[64,128,8,64]{3,0,2,1:T(8,128)(2,1)} %copy.49), kind=kOutput, calls=%fused_computation.28 | convolution fusion | flops 68149248 | bytes 11567104 | tf_op jit(solution)/shard_map/mthc,nthc->thmn/dot_general | solution.py:47
  640.3 3.8 fusion.32
  644.1 9.4 %fusion.29 = bf16[8,128,8,64]{3,0,2,1:T(8,128)(2,1)} fusion(bf16[64,128,8,64]{3,0,2,1:T(8,128)(2,1)} %copy.50, f32[128,8,8,64]{3,2,1,0:T(8,128)S(1)} %get-tuple-element.36, f32[8,128,8]{0,2,1:T(8,128)} %bitcast.88, f32[128,8,8]{2,1,0:T(8,128)} %copy-done.2), kind=kOutput, calls=%fused_computation.25 | convolution fusion | flops 69730304 | bytes 11599872 | tf_op jit(solution)/shard_map/thmn,nthc->mthc/dot_general | solution.py:53
  653.5 3.2 copy.51
  656.8 3.2 fusion.42
  659.9 8.0 %fusion.45 = bf16[8,128,512]{2,1,0:T(8,128)(2,1)} fusion(bf16[8,128,512]{2,1,0:T(8,128)(2,1)} %get-tuple-element.38, bf16[2048,512]{1,0:T(8,128)(2,1)S(1)} %copy-done, bf16[512,2048]{1,0:T(8,128)(2,1)} %param.20, f32[512]{0:T(512)S(1)} %copy-done.6, f32[8,128]{1,0:T(8,128)S(1)} %add_rsqrt_fusion), kind=kOutput, calls=%fused_computation.53 | convolution fusion | flops 4317511680 | bytes 6297600 | tf_op jit(solution)/shard_map/dot_general | solution.py:17
  (22 shorter events, 2.2 us)
Async XLA Ops:
  6.5 653.4 %copy-start = (bf16[2048,512]{1,0:T(8,128)(2,1)S(1)}, bf16[2048,512]{1,0:T(8,128)(2,1)}, u32[]{:S(2)}) copy-start(bf16[2048,512]{1,0:T(8,128)(2,1)} %param.21) | copy-start | bytes 6291460
  6.5 5.8 copy-start.3
  6.5 5.8 copy-start.4
  15.9 48.7 %all-to-all-start = ((bf16[16,4,128,192]{2,3,1,0:T(8,128)(2,1)}), bf16[16,4,128,192]{2,3,1,0:T(8,128)(2,1)}, u32[]{:S(2)}, u32[]{:S(2)}) async-start(bf16[16,4,128,192]{2,3,1,0:T(8,128)(2,1)} %bitcast.84), calls=%async_computation | async-start | bytes 6291456 | tf_op jit(solution)/shard_map/all_to_all | solution.py:88
  23.9 519.4 %all-gather.2.cloned.1.call-start = ((), (), s32[]{:S(2)}) async-start(), calls=%async_computation.2 | async-start | bytes 18874368 | tf_op jit(solution)/shard_map/all_gather | solution.py:101
  208.6 5.1 copy-start.5
  213.7 3.7 copy-start.7
  217.3 1.7 copy-start.1
  639.5 0.8 copy-start.2
  653.5 6.4 copy-start.6
Sparse Core Ops, SparseCore 0:
  220.8 322.4 all-gather.1
where the time goes:
time: 678 us; the launch traced here: 675 us
  waiting for transfers between devices  356 us (53%)
  local copies, waits for them, and re-layouts  132 us (19%)
  matrix products  105 us (15%)
  other arithmetic  39.6 us (6%)
  blocking collectives  21.3 us (3%)
  between operations  13.5 us (2%)
  starting transfers between devices  8.05 us (1%)
    all_gather x1, waiting for transfers between devices, per_device(): lax.all_gather(qkv_member[..., model_width:], 'mem', axis=0, tiled=True)  315 us
    unnamed x22, local copies, waits for them, and re-layouts  41.6 us
    all_to_all x1, waiting for transfers between devices, per_device(): lax.all_to_all(grouped_pairs, 'seq', split_axis=0, concat_axis=2, tiled=T...  40.6 us
    reduce_sum x4, other arithmetic, space_single(): totals = jnp.sum(weights, axis=-1, keepdims=True)  34.2 us
    dot_general x4, matrix products, space_single(): jnp.einsum('qc,kc->qk', queries, keys_here, preferred_element_type=jnp.fl...  32.4 us
    dot_general x4, matrix products, space_single(): jnp.dot(weights.astype(jnp.bfloat16), values, preferred_element_type=jnp....  29.7 us
    reshape x1, local copies, waits for them, and re-layouts, member_attend(): key_value[..., model_width:].reshape(others, tokens_here, HEADS, head_dim)  24 us
    reshape x1, local copies, waits for them, and re-layouts, member_attend(): key_value[..., :model_width].reshape(others, tokens_here, HEADS, head_dim)  24 us
  transfers between devices with their start and end apart: 2, of which 2 were waited for; matrix products, arithmetic and copies ran while one was open for 1% of the time, Pallas kernels for 0%

commit v1 on v0

v1 whole, which is shorter than its diff:
```python
import functools
import math

import jax
import jax.numpy as jnp
from jax import lax
from jax.experimental import pallas as pl
from jax.experimental.pallas import tpu as pltpu
from jax.sharding import Mesh, PartitionSpec as P

HEADS = 8
LANES = 128
SCORE_SCALE = math.log2(math.e)
VMEM_LIMIT = 48 * 1024 * 1024
NT = (((1,), (1,)), ((), ()))


def params():
    return pltpu.CompilerParams(vmem_limit_bytes=VMEM_LIMIT)


def normed(values, gain):
    scaled = values * lax.rsqrt(jnp.mean(values * values, axis=-1, keepdims=True) + 1e-05)
    return (scaled * gain).astype(jnp.bfloat16)


def dot(a, b):
    return jnp.dot(a, b, preferred_element_type=jnp.float32)


def lane_is_low(shape):
    return lax.broadcasted_iota(jnp.int32, shape, 1) < LANES // 2


def qkv_kernel(x_ref, gain_ref, w_ref, q_ref, k_ref, v_ref):
    width = x_ref.shape[-1]
    scale = (width // HEADS) ** (-0.5) * SCORE_SCALE
    rows = normed(x_ref[...].astype(jnp.float32), gain_ref[...])
    qkv = dot(rows, w_ref[...])
    q_ref[...] = (qkv[:, :width] * scale).astype(jnp.bfloat16)
    k_ref[...] = qkv[:, width : 2 * width].astype(jnp.bfloat16)
    v_ref[...] = qkv[:, 2 * width :].astype(jnp.bfloat16)


def project_qkv(x, gain, w, block=256):
    rows, width = x.shape
    row_spec = pl.BlockSpec((block, width), lambda i: (i, 0))
    return pl.pallas_call(
        qkv_kernel,
        grid=(rows // block,),
        in_specs=[
            row_spec,
            pl.BlockSpec((1, width), lambda i: (0, 0)),
            pl.BlockSpec((width, 3 * width), lambda i: (0, 0)),
        ],
        out_specs=[row_spec] * 3,
        out_shape=[jax.ShapeDtypeStruct((rows, width), jnp.bfloat16)] * 3,
        compiler_params=params(),
        name="space_qkv",
    )(x, gain, w)


def attend_kernel(q_ref, k0_ref, k1_ref, v0_ref, v1_ref, x_ref, w_ref, o_ref, kt, vz, att):
    half, width = k0_ref.shape
    head_dim = width // HEADS

    @pl.when(pl.program_id(0) == 0)
    def _():
        for part, (k_ref, v_ref) in enumerate(((k0_ref, v0_ref), (k1_ref, v1_ref))):
            kt[:, part * half : (part + 1) * half] = k_ref[...].T
            for pair in range(HEADS // 2):
                values = v_ref[:, pair * LANES : (pair + 1) * LANES]
                low = lane_is_low(values.shape)
                one = jnp.ones_like(values)
                vz[2 * pair, part * half : (part + 1) * half, :] = jnp.where(low, values, one)
                vz[2 * pair + 1, part * half : (part + 1) * half, :] = jnp.where(low, one, values)

    rows = q_ref.shape[0]
    low = lane_is_low((rows, LANES))
    for pair in range(HEADS // 2):
        lanes = slice(pair * LANES, (pair + 1) * LANES)
        queries = q_ref[:, lanes]
        none = jnp.zeros_like(queries)
        parts = []
        for odd in range(2):
            mine = jnp.where(low, none, queries) if odd else jnp.where(low, queries, none)
            scores = dot(mine, kt[lanes, :])
            peaks = jnp.max(scores, axis=-1, keepdims=True)
            weights = jnp.exp2(scores - peaks).astype(jnp.bfloat16)
            mixed = dot(weights, vz[2 * pair + odd])
            parts.append(mixed / pltpu.roll(mixed, LANES // 2, 1))
        att[:, lanes] = jnp.where(low, parts[0], parts[1]).astype(jnp.bfloat16)
    o_ref[...] = (x_ref[...].astype(jnp.float32) + dot(att[...], w_ref[...])).astype(jnp.bfloat16)


def attend(q, k0, k1, v0, v1, x, w, block=256):
    rows, width = q.shape
    keys = k0.shape[0]
    row_spec = pl.BlockSpec((block, width), lambda i: (i, 0))
    key_spec = pl.BlockSpec((keys, width), lambda i: (0, 0))
    return pl.pallas_call(
        attend_kernel,
        grid=(rows // block,),
        in_specs=[row_spec] + [key_spec] * 4 + [row_spec, pl.BlockSpec((width, width), lambda i: (0, 0))],
        out_specs=row_spec,
        out_shape=jax.ShapeDtypeStruct((rows, width), jnp.bfloat16),
        scratch_shapes=[
            pltpu.VMEM((width, 2 * keys), jnp.bfloat16),
            pltpu.VMEM((HEADS, 2 * keys, LANES), jnp.bfloat16),
            pltpu.VMEM((block, width), jnp.bfloat16),
        ],
        compiler_params=params(),
        name="space_attend",
    )(q, k0, k1, v0, v1, x, w)


def member_kernel(
    group, x_ref, gain_ref, wqkv_ref, wout_ref, gain2_ref, wup_ref, wdown_ref, o_ref, xf, of, att
):
    members, tokens, width = x_ref.shape
    scale = (width // HEADS) ** (-0.5) * SCORE_SCALE
    step = pl.program_id(0)

    @pl.when(step == 0)
    def _():
        flat = x_ref[...].reshape(members * tokens, width).astype(jnp.float32)
        for c in range(width // LANES):
            xf[c] = flat[:, c * LANES : (c + 1) * LANES]

    rows = group * members
    lines = [
        jnp.concatenate(
            [xf[c, pl.ds(step * group + t, members, stride=tokens), :] for c in range(width // LANES)],
            axis=1,
        )
        for t in range(group)
    ]
    x = jnp.concatenate(lines, axis=0)
    qkv = dot(normed(x, gain_ref[...]), wqkv_ref[...])
    low = lane_is_low((rows, LANES))
    same = (
        lax.broadcasted_iota(jnp.int32, (rows, rows), 0) // members
        == lax.broadcasted_iota(jnp.int32, (rows, rows), 1) // members
    )
    for pair in range(HEADS // 2):
        lo, hi = pair * LANES, (pair + 1) * LANES
        queries = (qkv[:, lo:hi] * scale).astype(jnp.bfloat16)
        keys = qkv[:, width + lo : width + hi].astype(jnp.bfloat16)
        values = qkv[:, 2 * width + lo : 2 * width + hi].astype(jnp.bfloat16)
        none, one = jnp.zeros_like(queries), jnp.ones_like(values)
        parts = []
        for odd in range(2):
            mine = jnp.where(low, none, queries) if odd else jnp.where(low, queries, none)
            scores = lax.dot_general(mine, keys, NT, preferred_element_type=jnp.float32)
            scores = jnp.where(same, scores, -jnp.inf)
            peaks = jnp.max(scores, axis=-1, keepdims=True)
            weights = jnp.exp2(scores - peaks).astype(jnp.bfloat16)
            mixed = dot(weights, jnp.where(low, one, values) if odd else jnp.where(low, values, one))
            parts.append(mixed / pltpu.roll(mixed, LANES // 2, 1))
        att[:, lo:hi] = jnp.where(low, parts[0], parts[1]).astype(jnp.bfloat16)
    after = (x + dot(att[...], wout_ref[...])).astype(jnp.bfloat16).astype(jnp.float32)
    up = dot(normed(after, gain2_ref[...]), wup_ref[...])
    hidden = jax.nn.gelu(up, approximate=True).astype(jnp.bfloat16)
    out = after + dot(hidden, wdown_ref[...])
    for t in range(group):
        for c in range(width // LANES):
            of[c, pl.ds(step * group + t, members, stride=tokens), :] = out[
                t * members : (t + 1) * members, c * LANES : (c + 1) * LANES
            ]

    @pl.when(step == pl.num_programs(0) - 1)
    def _():
        for c in range(width // LANES):
            o_ref[:, :, c * LANES : (c + 1) * LANES] = (
                of[c].astype(jnp.bfloat16).reshape(members, tokens, LANES)
            )


def member_part(x, gain, wqkv, wout, gain2, wup, wdown, group=4):
    members, tokens, width = x.shape
    ff = wup.shape[1]

    def whole(*shape):
        return pl.BlockSpec(shape, lambda i: (0,) * len(shape))

    return pl.pallas_call(
        functools.partial(member_kernel, group),
        grid=(tokens // group,),
        in_specs=[
            whole(members, tokens, width),
            whole(1, width),
            whole(width, 3 * width),
            whole(width, width),
            whole(1, width),
            whole(width, ff),
            whole(ff, width),
        ],
        out_specs=whole(members, tokens, width),
        out_shape=jax.ShapeDtypeStruct((members, tokens, width), jnp.bfloat16),
        scratch_shapes=[
            pltpu.VMEM((width // LANES, members * tokens, LANES), jnp.float32),
            pltpu.VMEM((width // LANES, members * tokens, LANES), jnp.float32),
            pltpu.VMEM((group * members, width), jnp.bfloat16),
        ],
        compiler_params=params(),
        name="member_part",
    )(x, gain, wqkv, wout, gain2, wup, wdown)


def per_device(
    state_field,
    gain_space,
    w_qkv_space,
    w_out_space,
    gain_member,
    w_qkv_member,
    w_out_member,
    gain_mlp,
    w_up,
    w_down,
):
    mem_dev, tok_dev, width = state_field.shape
    n_mem, n_grp = lax.axis_size("mem"), lax.axis_size("grp")
    gain_space, gain_member, gain_mlp = (g[None] for g in (gain_space, gain_member, gain_mlp))
    with jax.named_scope("tokens_to_member"):
        mine = lax.all_to_all(state_field, "grp", split_axis=0, concat_axis=0, tiled=True)
    x = mine.reshape(n_grp * tok_dev, width)
    q, k, v = project_qkv(x, gain_space, w_qkv_space)
    with jax.named_scope("keys_of_other_core"):
        k_other, v_other = (lax.ppermute(a, "core", [(0, 1), (1, 0)]) for a in (k, v))
    after_space = attend(q, k, k_other, v, v_other, x, w_out_space)
    here = tok_dev // n_mem
    sent = after_space.reshape(n_grp * n_mem, here, width)
    with jax.named_scope("members_to_tokens"):
        tokens = lax.all_to_all(sent, ("grp", "mem"), split_axis=0, concat_axis=0, tiled=True)
    out = member_part(
        tokens, gain_member, w_qkv_member, w_out_member, gain_mlp, w_up, w_down
    )
    out = out.reshape(n_grp, n_mem, here, width).transpose(1, 0, 2, 3)
    with jax.named_scope("tokens_back"):
        back = lax.all_to_all(out, "mem", split_axis=0, concat_axis=0, tiled=True)
    return back.transpose(1, 0, 2, 3).reshape(mem_dev, tok_dev, width)


def solution(mesh):
    grid = Mesh(mesh.devices.reshape(8, 8, 2), ("mem", "grp", "core"))
    rows = P("mem", ("grp", "core"), None)
    return jax.shard_map(
        per_device, mesh=grid, in_specs=(rows,) + (P(),) * 9, out_specs=rows, check_vma=False
    )
```

time: 678 us -> 127 us (0.19)
  waiting for transfers between devices: 356 us -> 3.65 us
  local copies, waits for them, and re-layouts: 132 us -> 2.15 us
  matrix products: 105 us -> 0 us
  Pallas kernels: 0 us -> 52.7 us
  blocking collectives: 21.3 us -> 67.9 us
  other arithmetic: 39.6 us -> 0 us
  between operations: 13.5 us -> 0.09 us
  starting transfers between devices: 8.05 us -> 0.58 us
    all_gather x1 -> x0, waiting for transfers between devices: 315 us -> none  [per_device(): lax.all_gather(qkv_member[..., model_width:], 'mem', axis=0, tiled=True)]
    dot_general x15 -> x0, matrix products: 105 us -> none  [the longest x4 32.4 us: space_single(): jnp.einsum('qc,kc->qk', queries, keys_here, preferred_element_type=jnp.fl...]
    pallas_call x0 -> x3, Pallas kernels: none -> 52.7 us  [the longest x1 27.6 us: attend(): pl.pallas_call(attend_kernel, grid=(rows // block,), in_specs=[row_spec]...]
    reshape x3 -> x1, local copies, waits for them, and re-layouts: 51.8 us -> 0.08 us  [per_device(): out = out.reshape(n_grp, n_mem, here, width).transpose(1, 0, 2, 3)]
    all_to_all x1 -> x3, blocking collectives: 21.3 us -> 67.9 us  [the longest x1 25.3 us: per_device(): lax.all_to_all(sent, ('grp', 'mem'), split_axis=0, concat_axis=0, tiled=T...]
    unnamed x22 -> x18, local copies, waits for them, and re-layouts: 41.6 us -> 1.01 us
    all_to_all x1 -> x0, waiting for transfers between devices: 40.6 us -> none  [per_device(): lax.all_to_all(grouped_pairs, 'seq', split_axis=0, concat_axis=2, tiled=T...]
    reduce_sum x6 -> x0, other arithmetic: 39.6 us -> none  [the longest x4 34.2 us: space_single(): totals = jnp.sum(weights, axis=-1, keepdims=True)]
  transfers between devices with their start and end apart: 2 -> 2, of which waited for: 2 -> 2; matrix products, arithmetic and copies ran while one was open for 1% -> 0% of each run, Pallas kernels for 0% -> 0%
where the time goes in v1:
time: 127 us
  blocking collectives  67.9 us (53%)
  Pallas kernels  52.7 us (41%)
  waiting for transfers between devices  3.65 us (3%)
  local copies, waits for them, and re-layouts  2.15 us (2%)
    pallas_call x1, Pallas kernels, attend(): pl.pallas_call(attend_kernel, grid=(rows // block,), in_specs=[row_spec]...  27.6 us
    all_to_all x1, blocking collectives, per_device(): lax.all_to_all(sent, ('grp', 'mem'), split_axis=0, concat_axis=0, tiled=T...  25.3 us
    all_to_all x1, blocking collectives, per_device(): lax.all_to_all(state_field, 'grp', split_axis=0, concat_axis=0, tiled=True)  25.2 us
    pallas_call x1, Pallas kernels, member_part(): pl.pallas_call(functools.partial(member_kernel, group), grid=(tokens // g...  22.4 us
    all_to_all x1, blocking collectives, per_device(): back = lax.all_to_all(out, 'mem', split_axis=0, concat_axis=0, tiled=True)  17.5 us
    ppermute x2, waiting for transfers between devices, per_device(): lax.ppermute(a, 'core', [(0, 1), (1, 0)])  3.65 us
    pallas_call x1, Pallas kernels, project_qkv(): pl.pallas_call(qkv_kernel, grid=(rows // block,), in_specs=[row_spec, pl....  2.6 us
  transfers between devices with their start and end apart: 2, of which 2 were waited for; matrix products, arithmetic and copies ran while one was open for 0% of the time, Pallas kernels for 0%

profile of v1, /device:TPU:0, one launch (start us, length us, event | category | flops | bytes accessed | tf_op | source)
XLA Modules:
  0.0 127.0 jit_solution(2411226368533581363)
XLA Ops:
  0.0 0.0 copy-start.1
  0.0 0.0 copy-start.5
  0.0 0.0 copy-start.3
  0.0 25.2 %all_to_all.15 = bf16[8,128,512]{2,1,0:T(8,128)(2,1)S(1)} all-to-all(bf16[8,128,512]{2,1,0:T(8,128)(2,1)} %param.10), channel_id=1, replica_groups=mesh['mem'=8,'grp'=8,'core'=2] {'grp'}, dimensions={0} | all-to-all | bytes 2097152 | tf_op jit(solution)/shard_map/tokens_to_member/all_to_all | solution.py:226
  25.2 0.0 copy-start
  25.2 0.0 copy-done.1
  25.2 0.0 copy-done.5
  25.2 2.6 %space_qkv.1 = (bf16[1024,512]{1,0:T(8,128)(2,1)S(1)}, bf16[1024,512]{1,0:T(8,128)(2,1)S(1)}, bf16[1024,512]{1,0:T(8,128)(2,1)S(1)}) custom-call(bf16[1024,512]{1,0:T(8,128)(2,1)S(1)} %bitcast.12, f32[1,512]{1,0:T(1,128)S(1)} %bitcast.16, bf16[512,1536]{1,0:T(8,128)(2,1)S(1)} %copy-done.1), custom_call_target="tpu_custom_call" | custom-call | tf_op jit(solution)/shard_map/space_qkv/pallas_call | solution.py:48
  27.8 0.1 collective-permute-start
  27.9 0.5 collective-permute-start.1
  28.4 2.1 %collective-permute-done.k1_ref = bf16[1024,512]{1,0:T(8,128)(2,1)S(1)} collective-permute-done((bf16[1024,512]{1,0:T(8,128)(2,1)S(1)}, bf16[1024,512]{1,0:T(8,128)(2,1)S(1)}, u32[]{:S(2)}, u32[]{:S(2)}) %collective-permute-start) | collective-permute-done | bytes 1048608 | tf_op jit(solution)/shard_map/keys_of_other_core/ppermute | solution.py:230
  30.6 1.5 %collective-permute-done.1.v1_ref = bf16[1024,512]{1,0:T(8,128)(2,1)S(1)} collective-permute-done((bf16[1024,512]{1,0:T(8,128)(2,1)S(1)}, bf16[1024,512]{1,0:T(8,128)(2,1)S(1)}, u32[]{:S(2)}, u32[]{:S(2)}) %collective-permute-start.1) | collective-permute-done | bytes 1048608 | tf_op jit(solution)/shard_map/keys_of_other_core/ppermute | solution.py:230
  32.1 0.0 copy-start.8
  32.1 0.0 copy-done
  32.1 1.0 copy-done.8
  33.0 0.0 copy-done.3
  33.0 27.6 %space_attend.1 = bf16[1024,512]{1,0:T(8,128)(2,1)S(1)} custom-call(bf16[1024,512]{1,0:T(8,128)(2,1)S(1)} %get-tuple-element.8.q_ref, bf16[1024,512]{1,0:T(8,128)(2,1)S(1)} %get-tuple-element.9.k0_ref, bf16[1024,512]{1,0:T(8,128)(2,1)S(1)} %collective-permute-done.k1_ref, bf16[1024,512]{1,0:T(8,128)(2,1)S(1)} %get-tuple-element.10.v0_ref, ...), custom_call_target="tpu_custom_call" | custom-call | tf_op jit(solution)/shard_map/space_attend/pallas_call | solution.py:101
  60.7 0.0 copy-start.2
  60.7 0.0 copy-start.4
  60.7 0.0 copy-start.6
  60.7 0.0 copy-start.7
  60.7 25.3 %all_to_all.16.x_ref = bf16[64,16,512]{2,1,0:T(8,128)(2,1)S(1)} all-to-all(bf16[64,16,512]{2,1,0:T(8,128)(2,1)S(1)} %bitcast.14), channel_id=1, replica_groups=mesh['mem'=8,'grp'=8,'core'=2] {'grp','mem'}, dimensions={0} | all-to-all | bytes 2097152 | tf_op jit(solution)/shard_map/members_to_tokens/all_to_all | solution.py:235
  86.0 0.0 copy-done.2
  86.0 0.0 copy-done.4
  86.0 0.0 copy-done.6
  86.0 0.0 copy-done.7
  86.0 22.4 %member_part.1 = bf16[64,16,512]{2,1,0:T(8,128)(2,1)S(1)} custom-call(bf16[64,16,512]{2,1,0:T(8,128)(2,1)S(1)} %all_to_all.16.x_ref, f32[1,512]{1,0:T(1,128)S(1)} %bitcast.17, bf16[512,1536]{1,0:T(8,128)(2,1)S(1)} %copy-done.2, bf16[512,512]{1,0:T(8,128)(2,1)S(1)} %copy-done.4, f32[1,512]{1,0:T(1,128)S(1)} %bitcast.18, bf16[512,2048]{1,0:T(8,128)(2,1)} %wup_ref.1, ...), custom_call_target="tpu_custom_call" | custom-call | tf_op jit(solution)/shard_map/member_part/pallas_call | solution.py:186
  108.4 0.1 copy.15
  108.5 17.5 %all_to_all.17 = bf16[8,8,16,512]{3,2,1,0:T(8,128)(2,1)S(1)} all-to-all(bf16[8,8,16,512]{3,2,1,0:T(8,128)(2,1)S(1)} %bitcast.19), channel_id=1, replica_groups=mesh['mem'=8,'grp'=8,'core'=2] {'mem'}, dimensions={0} | all-to-all | bytes 2097152 | tf_op jit(solution)/shard_map/tokens_back/all_to_all | solution.py:241
  126.0 1.1 copy.13
Async XLA Ops:
  0.0 25.2 %copy-start.1 = (bf16[512,1536]{1,0:T(8,128)(2,1)S(1)}, bf16[512,1536]{1,0:T(8,128)(2,1)}, u32[]{:S(2)}) copy-start(bf16[512,1536]{1,0:T(8,128)(2,1)} %w_ref.2) | copy-start | bytes 4718596
  0.0 25.2 %copy-start.5 = (f32[512]{0:T(512)S(1)}, f32[512]{0:T(512)}, u32[]{:S(2)}) copy-start(f32[512]{0:T(512)} %param.11) | copy-start | bytes 6148
  0.0 33.0 %copy-start.3 = (bf16[512,512]{1,0:T(8,128)(2,1)S(1)}, bf16[512,512]{1,0:T(8,128)(2,1)}, u32[]{:S(2)}) copy-start(bf16[512,512]{1,0:T(8,128)(2,1)} %w_ref.3) | copy-start | bytes 1572868
  25.2 6.9 %copy-start = (bf16[8,128,512]{2,1,0:T(8,128)(2,1)}, bf16[8,128,512]{2,1,0:T(8,128)(2,1)S(1)}, u32[]{:S(2)}) copy-start(bf16[8,128,512]{2,1,0:T(8,128)(2,1)S(1)} %all_to_all.15) | copy-start | bytes 3145732
  27.8 2.7 %collective-permute-start = (bf16[1024,512]{1,0:T(8,128)(2,1)S(1)}, bf16[1024,512]{1,0:T(8,128)(2,1)S(1)}, u32[]{:S(2)}, u32[]{:S(2)}) collective-permute-start(bf16[1024,512]{1,0:T(8,128)(2,1)S(1)} %get-tuple-element.9.k0_ref), channel_id=1, source_target_pairs={{0,1},{1,0},{2,3},{3,2},{4,5},{5,4},{6,7},{7,6},{8,9},{9,8},{10,11... | collective-permute-start | bytes 3145736 | tf_op jit(solution)/shard_map/keys_of_other_core/ppermute | solution.py:230
  27.9 4.1 %collective-permute-start.1 = (bf16[1024,512]{1,0:T(8,128)(2,1)S(1)}, bf16[1024,512]{1,0:T(8,128)(2,1)S(1)}, u32[]{:S(2)}, u32[]{:S(2)}) collective-permute-start(bf16[1024,512]{1,0:T(8,128)(2,1)S(1)} %get-tuple-element.10.v0_ref), channel_id=1, source_target_pairs={{0,1},{1,0},{2,3},{3,2},{4,5},{5,4},{6,7},{7,6},{8,9},{9,8},{10,11... | collective-permute-start | bytes 3145736 | tf_op jit(solution)/shard_map/keys_of_other_core/ppermute | solution.py:230
  32.1 1.0 copy-start.8
  60.7 25.3 %copy-start.2 = (bf16[512,1536]{1,0:T(8,128)(2,1)S(1)}, bf16[512,1536]{1,0:T(8,128)(2,1)}, u32[]{:S(2)}) copy-start(bf16[512,1536]{1,0:T(8,128)(2,1)} %wqkv_ref.1) | copy-start | bytes 4718596
  60.7 25.3 %copy-start.4 = (bf16[512,512]{1,0:T(8,128)(2,1)S(1)}, bf16[512,512]{1,0:T(8,128)(2,1)}, u32[]{:S(2)}) copy-start(bf16[512,512]{1,0:T(8,128)(2,1)} %wout_ref.1) | copy-start | bytes 1572868
  60.7 25.3 %copy-start.6 = (f32[512]{0:T(512)S(1)}, f32[512]{0:T(512)}, u32[]{:S(2)}) copy-start(f32[512]{0:T(512)} %param.14) | copy-start | bytes 6148
  60.7 25.3 %copy-start.7 = (f32[512]{0:T(512)S(1)}, f32[512]{0:T(512)}, u32[]{:S(2)}) copy-start(f32[512]{0:T(512)} %param.17) | copy-start | bytes 6148

commit v2 on v1

v2 whole, which is shorter than its diff:
```python
import functools
import math

import jax
import jax.numpy as jnp
from jax import lax
from jax.experimental import pallas as pl
from jax.experimental.pallas import tpu as pltpu
from jax.sharding import Mesh, PartitionSpec as P

HEADS = 8
LANES = 128
SCORE_SCALE = math.log2(math.e)
VMEM_LIMIT = 24 * 1024 * 1024
NT = (((1,), (1,)), ((), ()))


def params():
    return pltpu.CompilerParams(vmem_limit_bytes=VMEM_LIMIT)


def cost(flops, moved):
    return pl.CostEstimate(flops=int(flops), bytes_accessed=int(moved), transcendentals=0)


def normed(values, gain):
    scaled = values * lax.rsqrt(jnp.mean(values * values, axis=-1, keepdims=True) + 1e-05)
    return (scaled * gain).astype(jnp.bfloat16)


def dot(a, b):
    return jnp.dot(a, b, preferred_element_type=jnp.float32)


def lane_is_low(shape):
    return lax.broadcasted_iota(jnp.int32, shape, 1) < LANES // 2


def qkv_kernel(want_q, x_ref, gain_ref, w_ref, *outs):
    width = x_ref.shape[-1]
    scale = (width // HEADS) ** (-0.5) * SCORE_SCALE
    q_ref, kt_ref, vz_ref = outs if want_q else (None,) + outs
    rows = normed(x_ref[...].astype(jnp.float32), gain_ref[...])
    if want_q:
        q_ref[...] = (dot(rows, w_ref[:, :width]) * scale).astype(jnp.bfloat16)
    kt_ref[...] = dot(rows, w_ref[:, width : 2 * width]).astype(jnp.bfloat16).T
    values = dot(rows, w_ref[:, 2 * width :]).astype(jnp.bfloat16)
    for pair in range(HEADS // 2):
        mine = values[:, pair * LANES : (pair + 1) * LANES]
        low = lane_is_low(mine.shape)
        one = jnp.ones_like(mine)
        vz_ref[2 * pair] = jnp.where(low, mine, one)
        vz_ref[2 * pair + 1] = jnp.where(low, one, mine)


def project_qkv(x, gain, w, want_q, block=256):
    rows, width = x.shape
    row_spec = pl.BlockSpec((block, width), lambda i: (i, 0))
    out_specs = [
        row_spec,
        pl.BlockSpec((width, block), lambda i: (0, i)),
        pl.BlockSpec((HEADS, block, LANES), lambda i: (0, i, 0)),
    ]
    out_shape = [
        jax.ShapeDtypeStruct((rows, width), jnp.bfloat16),
        jax.ShapeDtypeStruct((width, rows), jnp.bfloat16),
        jax.ShapeDtypeStruct((HEADS, rows, LANES), jnp.bfloat16),
    ]
    return pl.pallas_call(
        functools.partial(qkv_kernel, want_q),
        grid=(rows // block,),
        in_specs=[
            row_spec,
            pl.BlockSpec((1, width), lambda i: (0, 0)),
            pl.BlockSpec((width, 3 * width), lambda i: (0, 0)),
        ],
        out_specs=out_specs if want_q else out_specs[1:],
        out_shape=out_shape if want_q else out_shape[1:],
        compiler_params=params(),
        cost_estimate=cost(2 * rows * width * width * (3 if want_q else 2), 6 * rows * width),
        name="space_qkv" if want_q else "space_kv",
    )(x, gain, w)


def attend_kernel(block, keys_step, q_ref, kt0, kt1, vz0, vz1, x_ref, w_ref, o_ref, held, att):
    rows = q_ref.shape[0]
    half = kt0.shape[1]
    steps = 2 * half // keys_step
    blocks = rows // block
    low = lane_is_low((block, LANES))

    def place(step):
        at = step % (steps // 2) * keys_step
        return step >= steps // 2, slice(at, at + keys_step)

    def head_queries(at, head):
        pair = head // 2
        queries = q_ref[pl.ds(at * block, block), pair * LANES : (pair + 1) * LANES]
        none = jnp.zeros_like(queries)
        return jnp.where(low, none, queries) if head % 2 else jnp.where(low, queries, none)

    def score(queries, head, step, slot, peak):
        second, cols = place(step)
        pair = head // 2
        keys = (kt1 if second else kt0)[pair * LANES : (pair + 1) * LANES, cols]
        scores = dot(queries, keys)
        held[slot, :, step * keys_step : (step + 1) * keys_step] = scores
        for c in range(keys_step // LANES):
            part = scores[:, c * LANES : (c + 1) * LANES]
            peak = part if peak is None else jnp.maximum(peak, part)
        return peak

    def mix(head, step, slot, peaks):
        second, cols = place(step)
        scores = held[slot, :, step * keys_step : (step + 1) * keys_step]
        weights = jnp.exp2(scores - peaks).astype(jnp.bfloat16)
        return dot(weights, (vz1 if second else vz0)[head, cols, :])

    def row_peaks(peak):
        return jnp.max(peak, axis=-1, keepdims=True)

    peak = None
    first = head_queries(0, 0)
    for step in range(steps):
        peak = score(first, 0, step, 0, peak)

    def body(at, peaks):
        even = None
        for head in range(HEADS):
            after = (head + 1) % HEADS
            queries = head_queries(at if after else jnp.minimum(at + 1, blocks - 1), after)
            peak, mixed = None, None
            for step in range(steps):
                part = mix(head, step, head % 2, peaks)
                mixed = part if mixed is None else mixed + part
                peak = score(queries, after, step, after % 2, peak)
            peaks = row_peaks(peak)
            mixed = mixed / pltpu.roll(mixed, LANES // 2, 1)
            if head % 2:
                pair = head // 2
                att[:, pair * LANES : (pair + 1) * LANES] = jnp.where(low, even, mixed).astype(
                    jnp.bfloat16
                )
            even = mixed
        here = pl.ds(at * block, block)
        out = x_ref[here, :].astype(jnp.float32) + dot(att[...], w_ref[...])
        o_ref[here, :] = out.astype(jnp.bfloat16)
        return peaks

    lax.fori_loop(0, blocks, body, row_peaks(peak))


def attend(q, kt0, kt1, vz0, vz1, x, w, block=512, keys_step=256):
    rows, width = q.shape
    keys = 2 * kt0.shape[1]
    in_vmem = pl.BlockSpec(memory_space=pltpu.VMEM)
    return pl.pallas_call(
        functools.partial(attend_kernel, block, keys_step),
        in_specs=[in_vmem] * 7,
        out_specs=in_vmem,
        out_shape=jax.ShapeDtypeStruct((rows, width), jnp.bfloat16),
        scratch_shapes=[
            pltpu.VMEM((2, block, keys), jnp.float32),
            pltpu.VMEM((block, width), jnp.bfloat16),
        ],
        compiler_params=params(),
        cost_estimate=cost(16 * rows * keys * width, 12 * keys * width),
        name="space_attend",
    )(q, kt0, kt1, vz0, vz1, x, w)


def member_kernel(
    block, ff_step, ahead, x_ref, gain_ref, wqkv_ref, wout_ref, gain2_ref, wup_ref, wdown_ref,
    o_ref, rows32, qs, ks, vs, att,
):
    members, tokens, width = x_ref.shape
    ff = wup_ref.shape[1]
    total = members * tokens
    scale = (width // HEADS) ** (-0.5) * SCORE_SCALE
    columns = range(width // LANES)
    flat = x_ref[...].reshape(total, width).astype(jnp.float32)
    for c in columns:
        rows32[c] = flat[:, c * LANES : (c + 1) * LANES]

    def lane_slice(c):
        return slice(c * LANES, (c + 1) * LANES)

    def token_rows(token):
        parts = [rows32[c, pl.ds(token, members, stride=tokens), :] for c in columns]
        return jnp.concatenate(parts, axis=1)

    per_block = block // members
    xs = []
    for b in range(total // block):
        here = slice(b * block, (b + 1) * block)
        x = jnp.concatenate([token_rows(b * per_block + t) for t in range(per_block)], axis=0)
        xs.append(x)
        n = normed(x, gain_ref[...])
        qs[here, :] = (dot(n, wqkv_ref[:, :width]) * scale).astype(jnp.bfloat16)
        ks[here, :] = dot(n, wqkv_ref[:, width : 2 * width]).astype(jnp.bfloat16)
        vs[here, :] = dot(n, wqkv_ref[:, 2 * width :]).astype(jnp.bfloat16)

    tile = 4 * members
    low = lane_is_low((tile, LANES))
    same = (
        lax.broadcasted_iota(jnp.int32, (tile, tile), 0) // members
        == lax.broadcasted_iota(jnp.int32, (tile, tile), 1) // members
    )
    work = [
        (slice(g * tile, (g + 1) * tile), lane_slice(h // 2), h % 2)
        for g in range(total // tile)
        for h in range(HEADS)
    ]

    def score(rows, lanes, odd):
        queries = qs[rows, lanes]
        none = jnp.zeros_like(queries)
        queries = jnp.where(low, none, queries) if odd else jnp.where(low, queries, none)
        return lax.dot_general(queries, ks[rows, lanes], NT, preferred_element_type=jnp.float32)

    pending = [score(*w) for w in work[:ahead]]
    even = None
    for i, (rows, lanes, odd) in enumerate(work):
        scores = pending.pop(0)
        if i + ahead < len(work):
            pending.append(score(*work[i + ahead]))
        scores = jnp.where(same, scores, -jnp.inf)
        peaks = jnp.max(scores, axis=-1, keepdims=True)
        weights = jnp.exp2(scores - peaks).astype(jnp.bfloat16)
        values = vs[rows, lanes]
        one = jnp.ones_like(values)
        mixed = dot(weights, jnp.where(low, one, values) if odd else jnp.where(low, values, one))
        mixed = mixed / pltpu.roll(mixed, LANES // 2, 1)
        if odd:
            att[rows, lanes] = jnp.where(low, even, mixed).astype(jnp.bfloat16)
        even = mixed

    for b in range(total // block):
        here = slice(b * block, (b + 1) * block)
        after = (xs[b] + dot(att[here, :], wout_ref[...])).astype(jnp.bfloat16).astype(jnp.float32)
        out = after
        n = normed(after, gain2_ref[...])
        up = dot(n, wup_ref[:, :ff_step])
        for j in range(0, ff, ff_step):
            later = dot(n, wup_ref[:, j + ff_step : j + 2 * ff_step]) if j + ff_step < ff else None
            hidden = jax.nn.gelu(up, approximate=True).astype(jnp.bfloat16)
            out = out + dot(hidden, wdown_ref[j : j + ff_step, :])
            up = later
        for t in range(per_block):
            for c in columns:
                rows32[c, pl.ds(b * per_block + t, members, stride=tokens), :] = out[
                    t * members : (t + 1) * members, lane_slice(c)
                ]
    for c in columns:
        o_ref[:, :, lane_slice(c)] = (
            rows32[c].astype(jnp.bfloat16).reshape(members, tokens, LANES)
        )


def member_part(x, gain, wqkv, wout, gain2, wup, wdown, block=256, ff_step=512, ahead=4):
    members, tokens, width = x.shape
    total, ff = members * tokens, wup.shape[1]
    in_vmem = pl.BlockSpec(memory_space=pltpu.VMEM)
    return pl.pallas_call(
        functools.partial(member_kernel, block, ff_step, ahead),
        in_specs=[in_vmem] * 7,
        out_specs=in_vmem,
        out_shape=jax.ShapeDtypeStruct((members, tokens, width), jnp.bfloat16),
        scratch_shapes=[pltpu.VMEM((width // LANES, total, LANES), jnp.float32)]
        + [pltpu.VMEM((total, width), jnp.bfloat16)] * 4,
        compiler_params=params(),
        cost_estimate=cost(total * width * 2 * (4 * width + 2 * ff) * 2, 6 * total * width),
        name="member_part",
    )(x, gain, wqkv, wout, gain2, wup, wdown)


def per_device(
    state_field,
    gain_space,
    w_qkv_space,
    w_out_space,
    gain_member,
    w_qkv_member,
    w_out_member,
    gain_mlp,
    w_up,
    w_down,
):
    mem_dev, tok_dev, width = state_field.shape
    n_mem, n_grp = lax.axis_size("mem"), lax.axis_size("grp")
    gain_space, gain_member, gain_mlp = (g[None] for g in (gain_space, gain_member, gain_mlp))
    with jax.named_scope("tokens_to_member"):
        mine = lax.all_to_all(state_field, "grp", split_axis=0, concat_axis=0, tiled=True)
    x = mine.reshape(n_grp * tok_dev, width)
    with jax.named_scope("rows_of_other_core"):
        x_other = lax.ppermute(x, "core", [(0, 1), (1, 0)])
    q, kt, vz = project_qkv(x, gain_space, w_qkv_space, True)
    kt_other, vz_other = project_qkv(x_other, gain_space, w_qkv_space, False)
    after_space = attend(q, kt, kt_other, vz, vz_other, x, w_out_space)
    here = tok_dev // n_mem
    sent = after_space.reshape(n_grp * n_mem, here, width)
    with jax.named_scope("members_to_tokens"):
        tokens = lax.all_to_all(sent, ("grp", "mem"), split_axis=0, concat_axis=0, tiled=True)
    out = member_part(tokens, gain_member, w_qkv_member, w_out_member, gain_mlp, w_up, w_down)
    out = out.reshape(n_grp, n_mem, here, width).transpose(1, 0, 2, 3)
    with jax.named_scope("tokens_back"):
        back = lax.all_to_all(out, "mem", split_axis=0, concat_axis=0, tiled=True)
    return back.transpose(1, 0, 2, 3).reshape(mem_dev, tok_dev, width)


def solution(mesh):
    grid = Mesh(mesh.devices.reshape(8, 8, 2), ("mem", "grp", "core"))
    rows = P("mem", ("grp", "core"), None)
    return jax.shard_map(
        per_device, mesh=grid, in_specs=(rows,) + (P(),) * 9, out_specs=rows, check_vma=False
    )
```

time: 127 us -> 109 us (0.86)
  Pallas kernels: 52.7 us -> 39 us
  waiting for transfers between devices: 3.65 us -> 0.01 us
    pallas_call x3 -> x4, Pallas kernels: 52.7 us -> 39 us  [the longest x1 19.3 us: attend(): pl.pallas_call(functools.partial(attend_kernel, block, keys_step), in_spe...]
    ppermute x2 -> x1, waiting for transfers between devices: 3.65 us -> 0.01 us  [per_device(): x_other = lax.ppermute(x, 'core', [(0, 1), (1, 0)])]
  transfers between devices with their start and end apart: 2 -> 1, of which waited for: 2 -> 0; matrix products, arithmetic and copies ran while one was open for 0% -> 0% of each run, Pallas kernels for 0% -> 3%
where the time goes in v2:
time: 109 us
  blocking collectives  68.5 us (63%)
  Pallas kernels  39 us (36%)
  local copies, waits for them, and re-layouts  1.2 us (1%)
    all_to_all x1, blocking collectives, per_device(): lax.all_to_all(sent, ('grp', 'mem'), split_axis=0, concat_axis=0, tiled=T...  25.7 us
    all_to_all x1, blocking collectives, per_device(): lax.all_to_all(state_field, 'grp', split_axis=0, concat_axis=0, tiled=True)  25.2 us
    pallas_call x1, Pallas kernels, attend(): pl.pallas_call(functools.partial(attend_kernel, block, keys_step), in_spe...  19.3 us
    all_to_all x1, blocking collectives, per_device(): back = lax.all_to_all(out, 'mem', split_axis=0, concat_axis=0, tiled=True)  17.7 us
    pallas_call x1, Pallas kernels, member_part(): pl.pallas_call(functools.partial(member_kernel, block, ff_step, ahead), i...  14.1 us
    pallas_call x2, Pallas kernels, project_qkv(): pl.pallas_call(functools.partial(qkv_kernel, want_q), grid=(rows // block...  5.6 us
  transfers between devices with their start and end apart: 1, of which 0 were waited for; matrix products, arithmetic and copies ran while one was open for 0% of the time, Pallas kernels for 3%

profile of v2, /device:TPU:0, one launch (start us, length us, event | category | flops | bytes accessed | tf_op | source)
XLA Modules:
  0.0 108.9 jit_solution(14314115352850320240)
XLA Ops:
  0.0 0.0 copy-start.2
  0.0 0.0 copy-start.6
  0.0 25.2 %all_to_all.15 = bf16[8,128,512]{2,1,0:T(8,128)(2,1)S(1)} all-to-all(bf16[8,128,512]{2,1,0:T(8,128)(2,1)} %param.10), channel_id=1, replica_groups=mesh['mem'=8,'grp'=8,'core'=2] {'grp'}, dimensions={0} | all-to-all | bytes 2097152 | tf_op jit(solution)/shard_map/tokens_to_member/all_to_all | solution.py:293
  25.2 0.0 collective-permute-start
  25.2 0.0 copy-done.2
  25.2 0.0 copy-done.6
  25.2 3.1 %space_qkv.1 = (bf16[1024,512]{1,0:T(8,128)(2,1)S(1)}, bf16[512,1024]{1,0:T(8,128)(2,1)S(1)}, bf16[8,1024,128]{2,1,0:T(8,128)(2,1)S(1)}) custom-call(bf16[1024,512]{1,0:T(8,128)(2,1)S(1)} %bitcast.13, f32[1,512]{1,0:T(1,128)S(1)} %bitcast.17, bf16[512,1536]{1,0:T(8,128)(2,1)S(1)} %copy-done.2), custom_call_target="tpu_custom_call" | custom-call | flops 1610612736 | bytes 3145728 | tf_op jit(solution)/shard_map/space_qkv/pallas_call | solution.py:69
  28.3 0.0 copy-start.4
  28.3 0.0 collective-permute-done.x_ref
  28.3 2.5 %space_kv.1 = (bf16[512,1024]{1,0:T(8,128)(2,1)S(1)}, bf16[8,1024,128]{2,1,0:T(8,128)(2,1)S(1)}) custom-call(bf16[1024,512]{1,0:T(8,128)(2,1)S(1)} %collective-permute-done.x_ref, f32[1,512]{1,0:T(1,128)S(1)} %bitcast.18, bf16[512,1536]{1,0:T(8,128)(2,1)S(1)} %copy-done.2), custom_call_target="tpu_custom_call" | custom-call | flops 1073741824 | bytes 3145728 | tf_op jit(solution)/shard_map/space_kv/pallas_call | solution.py:69
  30.8 0.0 copy-done.4
  30.8 0.0 copy-start.1
  30.9 0.0 copy-start.3
  30.9 0.0 copy-start.5
  30.9 19.3 %space_attend.1 = bf16[1024,512]{1,0:T(8,128)(2,1)S(1)} custom-call(bf16[1024,512]{1,0:T(8,128)(2,1)S(1)} %get-tuple-element.10.q_ref, bf16[512,1024]{1,0:T(8,128)(2,1)S(1)} %get-tuple-element.11.kt0, bf16[512,1024]{1,0:T(8,128)(2,1)S(1)} %get-tuple-element.12.kt1, bf16[8,1024,128]{2,1,0:T(8,128)(2,1)S(1)} %get-tuple-element.13.vz0, ...), custom_call_target="tpu_custom_call" | custom-call | flops 17179869184 | bytes 12582912 | tf_op jit(solution)/shard_map/space_attend/pallas_call | solution.py:157
  50.2 0.0 copy-start
  50.2 0.0 copy-start.7
  50.2 0.0 copy-start.8
  50.3 25.7 %all_to_all.16.x_ref = bf16[64,16,512]{2,1,0:T(8,128)(2,1)S(1)} all-to-all(bf16[64,16,512]{2,1,0:T(8,128)(2,1)S(1)} %bitcast.15), channel_id=1, replica_groups=mesh['mem'=8,'grp'=8,'core'=2] {'grp','mem'}, dimensions={0} | all-to-all | bytes 2097152 | tf_op jit(solution)/shard_map/members_to_tokens/all_to_all | solution.py:303
  75.9 0.0 copy-done.1
  75.9 0.0 copy-done.3
  76.0 0.0 copy-done.5
  76.0 0.0 copy-done
  76.0 0.0 copy-done.7
  76.0 0.0 copy-done.8
  76.0 14.1 %member_part.1 = bf16[64,16,512]{2,1,0:T(8,128)(2,1)S(1)} custom-call(bf16[64,16,512]{2,1,0:T(8,128)(2,1)S(1)} %all_to_all.16.x_ref, f32[1,512]{1,0:T(1,128)S(1)} %bitcast.19, bf16[512,1536]{1,0:T(8,128)(2,1)S(1)} %copy-done.3, bf16[512,512]{1,0:T(8,128)(2,1)S(1)} %copy-done.5, f32[1,512]{1,0:T(1,128)S(1)} %bitcast.20, bf16[512,2048]{1,0:T(8,128)(2,1)S(1)} %copy-done, ...), custom_call_target="tpu_custom_call" | custom-call | flops 12884901888 | bytes 3145728 | tf_op jit(solution)/shard_map/member_part/pallas_call | solution.py:264
  90.1 0.1 copy.15
  90.2 17.7 %all_to_all.17 = bf16[8,8,16,512]{3,2,1,0:T(8,128)(2,1)S(1)} all-to-all(bf16[8,8,16,512]{3,2,1,0:T(8,128)(2,1)S(1)} %bitcast.21), channel_id=1, replica_groups=mesh['mem'=8,'grp'=8,'core'=2] {'mem'}, dimensions={0} | all-to-all | bytes 2097152 | tf_op jit(solution)/shard_map/tokens_back/all_to_all | solution.py:307
  107.8 1.1 copy.13
Async XLA Ops:
  0.0 25.2 %copy-start.2 = (bf16[512,1536]{1,0:T(8,128)(2,1)S(1)}, bf16[512,1536]{1,0:T(8,128)(2,1)}, u32[]{:S(2)}) copy-start(bf16[512,1536]{1,0:T(8,128)(2,1)} %w_ref.4) | copy-start | bytes 4718596
  0.0 25.2 %copy-start.6 = (f32[512]{0:T(512)S(1)}, f32[512]{0:T(512)}, u32[]{:S(2)}) copy-start(f32[512]{0:T(512)} %param.11) | copy-start | bytes 6148
  25.2 3.1 %collective-permute-start = (bf16[1024,512]{1,0:T(8,128)(2,1)S(1)}, bf16[1024,512]{1,0:T(8,128)(2,1)S(1)}, u32[]{:S(2)}, u32[]{:S(2)}) collective-permute-start(bf16[1024,512]{1,0:T(8,128)(2,1)S(1)} %bitcast.12), channel_id=1, source_target_pairs={{0,1},{1,0},{2,3},{3,2},{4,5},{5,4},{6,7},{7,6},{8,9},{9,8},{10,11... | collective-permute-start | bytes 3145736 | tf_op jit(solution)/shard_map/rows_of_other_core/ppermute | solution.py:296
  28.3 2.5 %copy-start.4 = (bf16[512,512]{1,0:T(8,128)(2,1)S(1)}, bf16[512,512]{1,0:T(8,128)(2,1)}, u32[]{:S(2)}) copy-start(bf16[512,512]{1,0:T(8,128)(2,1)} %w_ref.5) | copy-start | bytes 1572868
  30.8 45.1 %copy-start.1 = (bf16[2048,512]{1,0:T(8,128)(2,1)S(1)}, bf16[2048,512]{1,0:T(8,128)(2,1)}, u32[]{:S(2)}) copy-start(bf16[2048,512]{1,0:T(8,128)(2,1)} %wdown_ref.1) | copy-start | bytes 6291460
  30.9 45.1 %copy-start.3 = (bf16[512,1536]{1,0:T(8,128)(2,1)S(1)}, bf16[512,1536]{1,0:T(8,128)(2,1)}, u32[]{:S(2)}) copy-start(bf16[512,1536]{1,0:T(8,128)(2,1)} %wqkv_ref.1) | copy-start | bytes 4718596
  30.9 45.1 %copy-start.5 = (bf16[512,512]{1,0:T(8,128)(2,1)S(1)}, bf16[512,512]{1,0:T(8,128)(2,1)}, u32[]{:S(2)}) copy-start(bf16[512,512]{1,0:T(8,128)(2,1)} %wout_ref.1) | copy-start | bytes 1572868
  50.2 25.7 %copy-start = (bf16[512,2048]{1,0:T(8,128)(2,1)S(1)}, bf16[512,2048]{1,0:T(8,128)(2,1)}, u32[]{:S(2)}) copy-start(bf16[512,2048]{1,0:T(8,128)(2,1)} %wup_ref.1) | copy-start | bytes 6291460
  50.2 25.7 %copy-start.7 = (f32[512]{0:T(512)S(1)}, f32[512]{0:T(512)}, u32[]{:S(2)}) copy-start(f32[512]{0:T(512)} %param.14) | copy-start | bytes 6148
  50.2 25.7 %copy-start.8 = (f32[512]{0:T(512)S(1)}, f32[512]{0:T(512)}, u32[]{:S(2)}) copy-start(f32[512]{0:T(512)} %param.17) | copy-start | bytes 6148

commit v3 on v2

v3 whole, which is shorter than its diff:
```python
import functools
import math

import jax
import jax.numpy as jnp
from jax import lax
from jax.experimental import pallas as pl
from jax.experimental.pallas import tpu as pltpu
from jax.sharding import Mesh, PartitionSpec as P

HEADS = 8
LANES = 128
SCORE_SCALE = math.log2(math.e)
SMALL = jnp.float8_e4m3fn
NT = (((1,), (1,)), ((), ()))


def params(mib):
    return pltpu.CompilerParams(vmem_limit_bytes=mib * 1024 * 1024)


def cost(flops, moved):
    return pl.CostEstimate(flops=int(flops), bytes_accessed=int(moved), transcendentals=0)


def normed(values, gain):
    scaled = values * lax.rsqrt(jnp.mean(values * values, axis=-1, keepdims=True) + 1e-05)
    return (scaled * gain).astype(jnp.bfloat16)


def dot(a, b):
    return jnp.dot(a, b, preferred_element_type=jnp.float32)


def lane_is_low(shape):
    return lax.broadcasted_iota(jnp.int32, shape, 1) < LANES // 2


def high_low(values):
    high = values.astype(SMALL).astype(jnp.bfloat16)
    return high, values - high


def turned(values):
    return jnp.concatenate([values[:, LANES // 2 :], values[:, : LANES // 2]], axis=1)


def put_queries(q_ref, here, q):
    for pair in range(HEADS // 2):
        high, low_part = high_low(q[:, pair * LANES : (pair + 1) * LANES].astype(jnp.bfloat16))
        low_part = low_part * 4
        quarter = high * 0.25
        first = lane_is_low(high.shape)
        even, odd = 2 * pair, 2 * pair + 1
        q_ref[even, here, :LANES] = jnp.where(first, high, turned(quarter)).astype(SMALL)
        q_ref[even, here, LANES:] = jnp.where(first, low_part, turned(low_part)).astype(SMALL)
        q_ref[odd, here, :LANES] = jnp.where(first, turned(high), quarter).astype(SMALL)
        q_ref[odd, here, LANES:] = jnp.where(first, turned(low_part), low_part).astype(SMALL)


def put_keys(kt_ref, here, k):
    high, low = high_low(k.astype(jnp.bfloat16).T)
    parts = [p.astype(SMALL) for p in (high, low * 4, high * 0.25, low * 0.25)]
    dim = high.shape[0] // HEADS
    for head in range(HEADS):
        for i, part in enumerate(parts):
            kt_ref[head, i * dim : (i + 1) * dim, here] = part[head * dim : (head + 1) * dim]


def qkv_kernel(want_q, block, x_ref, gain_ref, w_ref, *outs):
    total, width = x_ref.shape
    q_scale = SCORE_SCALE * 2 * (width // HEADS) ** (-0.5)
    for b in range(total // block):
        here = slice(b * block, (b + 1) * block)
        rows = normed(x_ref[here, :].astype(jnp.float32), gain_ref[...])
        if want_q:
            put_queries(outs[0], here, dot(rows, w_ref[:, :width]) * q_scale)
        put_keys(outs[-2], here, dot(rows, w_ref[:, width : 2 * width]) * 0.5)
        outs[-1][here, :] = dot(rows, w_ref[:, 2 * width :]).astype(jnp.bfloat16)


def project_qkv(x, gain, w, want_q, block=512):
    rows, width = x.shape
    in_vmem = pl.BlockSpec(memory_space=pltpu.VMEM)
    out_shape = [
        jax.ShapeDtypeStruct((HEADS, rows, 2 * LANES), SMALL),
        jax.ShapeDtypeStruct((HEADS, 2 * LANES, rows), SMALL),
        jax.ShapeDtypeStruct((rows, width), jnp.bfloat16),
    ]
    out_shape = out_shape if want_q else out_shape[1:]
    return pl.pallas_call(
        functools.partial(qkv_kernel, want_q, block),
        in_specs=[in_vmem] * 3,
        out_specs=[in_vmem] * len(out_shape),
        out_shape=out_shape,
        compiler_params=params(12),
        cost_estimate=cost(2 * rows * width * width * (3 if want_q else 2), 6 * rows * width),
        name="space_qkv" if want_q else "space_kv",
    )(x, gain, w)


def attend_kernel(
    block, keys_step, q_ref, kt0, kt1, v0_ref, v1_ref, x_ref, w_ref, o_ref, held, att
):
    rows = x_ref.shape[0]
    half = v0_ref.shape[0]
    steps = 2 * half // keys_step
    pairs = HEADS // 2
    units = rows // block * pairs
    low = lane_is_low((block, LANES))
    ones = jnp.ones((keys_step, LANES), jnp.bfloat16)
    tops = {}

    def place(at):
        unit, step = divmod(at, steps)
        b, pair = divmod(unit, pairs)
        key_at = step % (steps // 2) * keys_step
        return (
            unit,
            step,
            slice(b * block, (b + 1) * block),
            pair,
            slice(pair * LANES, (pair + 1) * LANES),
            step >= steps // 2,
            slice(key_at, key_at + keys_step),
            slice(step * keys_step, (step + 1) * keys_step),
        )

    def score(at):
        unit, step, here, pair, _, second, keys, cols = place(at)
        kt = kt1 if second else kt0
        for odd in range(2):
            scores = dot(q_ref[2 * pair + odd, here], kt[2 * pair + odd, :, keys])
            held[unit % 2, odd * block : (odd + 1) * block, cols] = scores
            top = tops.get((unit, odd))
            for c in range(keys_step // LANES):
                part = scores[:, c * LANES : (c + 1) * LANES]
                top = part if top is None else jnp.maximum(top, part)
            tops[unit, odd] = top if step < steps - 1 else jnp.max(top, axis=-1, keepdims=True)

    def mix(at):
        unit, _, _, _, lanes, second, keys, cols = place(at)
        weights = [
            jnp.exp2(held[unit % 2, odd * block : (odd + 1) * block, cols] - tops[unit, odd])
            for odd in range(2)
        ]
        values = (v1_ref if second else v0_ref)[keys, lanes]
        return dot(
            jnp.concatenate([w.astype(jnp.bfloat16) for w in weights], axis=0),
            jnp.concatenate([values, ones], axis=1),
        )

    for at in range(steps):
        score(at)
    mixed = None
    for at in range(units * steps):
        unit, step, here, pair, lanes, _, _, _ = place(at)
        part = mix(at)
        mixed = mixed + part if step else part
        if at + steps < units * steps:
            score(at + steps)
        if step == steps - 1:
            done = mixed[:, :LANES] / mixed[:, LANES:]
            att[here, lanes] = jnp.where(low, done[:block], done[block:]).astype(jnp.bfloat16)
            if pair == pairs - 1:
                out = x_ref[here, :].astype(jnp.float32) + dot(att[here, :], w_ref[...])
                o_ref[here, :] = out.astype(jnp.bfloat16)


def attend(q, kt0, kt1, v0, v1, x, w, block=512, keys_step=512):
    rows, width = x.shape
    keys = 2 * v0.shape[0]
    in_vmem = pl.BlockSpec(memory_space=pltpu.VMEM)
    return pl.pallas_call(
        functools.partial(attend_kernel, block, keys_step),
        in_specs=[in_vmem] * 7,
        out_specs=in_vmem,
        out_shape=jax.ShapeDtypeStruct((rows, width), jnp.bfloat16),
        scratch_shapes=[
            pltpu.VMEM((2, 2 * block, keys), jnp.float32),
            pltpu.VMEM((rows, width), jnp.bfloat16),
        ],
        compiler_params=params(28),
        cost_estimate=cost(8 * rows * keys * width, 12 * keys * width),
        name="space_attend",
    )(q, kt0, kt1, v0, v1, x, w)


def member_kernel(
    block, mlp_block, ff_step, x_ref, gain_ref, wqkv_ref, wout_ref, gain2_ref, wup_ref, wdown_ref,
    o_ref, rows32, qs, ks, vs, att,
):
    members, tokens, width = x_ref.shape
    ff = wup_ref.shape[1]
    total = members * tokens
    scale = (width // HEADS) ** (-0.5) * SCORE_SCALE
    columns = range(width // LANES)
    flat = x_ref[...].reshape(total, width).astype(jnp.float32)
    for c in columns:
        rows32[c] = flat[:, c * LANES : (c + 1) * LANES]

    def lane_slice(c):
        return slice(c * LANES, (c + 1) * LANES)

    def token_rows(token):
        parts = [rows32[c, pl.ds(token, members, stride=tokens), :] for c in columns]
        return jnp.concatenate(parts, axis=1)

    xs = []
    per_block = block // members
    for b in range(total // block):
        here = slice(b * block, (b + 1) * block)
        x = jnp.concatenate([token_rows(b * per_block + t) for t in range(per_block)], axis=0)
        xs.append(x)
        n = normed(x, gain_ref[...])
        qs[here, :] = (dot(n, wqkv_ref[:, :width]) * scale).astype(jnp.bfloat16)
        ks[here, :] = dot(n, wqkv_ref[:, width : 2 * width]).astype(jnp.bfloat16)
        vs[here, :] = dot(n, wqkv_ref[:, 2 * width :]).astype(jnp.bfloat16)

    tile = 4 * members
    low = lane_is_low((tile, LANES))
    same = (
        lax.broadcasted_iota(jnp.int32, (2 * tile, tile), 0) % tile // members
        == lax.broadcasted_iota(jnp.int32, (2 * tile, tile), 1) // members
    )
    ones = jnp.ones((tile, LANES), jnp.bfloat16)

    def score(rows, lanes):
        queries = qs[rows, lanes]
        none = jnp.zeros_like(queries)
        both = jnp.concatenate(
            [jnp.where(low, queries, none), jnp.where(low, none, queries)], axis=0
        )
        return lax.dot_general(both, ks[rows, lanes], NT, preferred_element_type=jnp.float32)

    work = [
        (slice(g * tile, (g + 1) * tile), lane_slice(pair))
        for g in range(total // tile)
        for pair in range(HEADS // 2)
    ]
    later = score(*work[0])
    for i, (rows, lanes) in enumerate(work):
        scores = jnp.where(same, later, -jnp.inf)
        if i + 1 < len(work):
            later = score(*work[i + 1])
        peaks = jnp.max(scores, axis=-1, keepdims=True)
        weights = jnp.exp2(scores - peaks).astype(jnp.bfloat16)
        mixed = dot(weights, jnp.concatenate([vs[rows, lanes], ones], axis=1))
        done = mixed[:, :LANES] / mixed[:, LANES:]
        att[rows, lanes] = jnp.where(low, done[:tile], done[tile:]).astype(jnp.bfloat16)

    for b in range(total // mlp_block):
        here = slice(b * mlp_block, (b + 1) * mlp_block)
        share = mlp_block // block
        x = jnp.concatenate(xs[b * share : (b + 1) * share], axis=0)
        after = (x + dot(att[here, :], wout_ref[...])).astype(jnp.bfloat16).astype(jnp.float32)
        out = after
        n = normed(after, gain2_ref[...])
        up = dot(n, wup_ref[:, :ff_step])
        for j in range(0, ff, ff_step):
            later = dot(n, wup_ref[:, j + ff_step : j + 2 * ff_step]) if j + ff_step < ff else None
            hidden = jax.nn.gelu(up, approximate=True).astype(jnp.bfloat16)
            out = out + dot(hidden, wdown_ref[j : j + ff_step, :])
            up = later
        for t in range(mlp_block // members):
            token = b * (mlp_block // members) + t
            for c in columns:
                rows32[c, pl.ds(token, members, stride=tokens), :] = out[
                    t * members : (t + 1) * members, lane_slice(c)
                ]
    for c in columns:
        o_ref[:, :, lane_slice(c)] = (
            rows32[c].astype(jnp.bfloat16).reshape(members, tokens, LANES)
        )


def member_part(x, gain, wqkv, wout, gain2, wup, wdown, block=256, mlp_block=512, ff_step=256):
    members, tokens, width = x.shape
    total, ff = members * tokens, wup.shape[1]
    in_vmem = pl.BlockSpec(memory_space=pltpu.VMEM)
    return pl.pallas_call(
        functools.partial(member_kernel, block, mlp_block, ff_step),
        in_specs=[in_vmem] * 7,
        out_specs=in_vmem,
        out_shape=jax.ShapeDtypeStruct((members, tokens, width), jnp.bfloat16),
        scratch_shapes=[pltpu.VMEM((width // LANES, total, LANES), jnp.float32)]
        + [pltpu.VMEM((total, width), jnp.bfloat16)] * 4,
        compiler_params=params(24),
        cost_estimate=cost(total * width * 2 * (4 * width + 2 * ff) * 2, 6 * total * width),
        name="member_part",
    )(x, gain, wqkv, wout, gain2, wup, wdown)


def per_device(
    state_field,
    gain_space,
    w_qkv_space,
    w_out_space,
    gain_member,
    w_qkv_member,
    w_out_member,
    gain_mlp,
    w_up,
    w_down,
):
    mem_dev, tok_dev, width = state_field.shape
    n_mem, n_grp = lax.axis_size("mem"), lax.axis_size("grp")
    gain_space, gain_member, gain_mlp = (g[None] for g in (gain_space, gain_member, gain_mlp))
    with jax.named_scope("tokens_to_member"):
        mine = lax.all_to_all(state_field, "grp", split_axis=0, concat_axis=0, tiled=True)
    x = mine.reshape(n_grp * tok_dev, width)
    with jax.named_scope("rows_of_other_core"):
        x_other = lax.ppermute(x, "core", [(0, 1), (1, 0)])
    q, kt, v = project_qkv(x, gain_space, w_qkv_space, True)
    kt_other, v_other = project_qkv(x_other, gain_space, w_qkv_space, False)
    after_space = attend(q, kt, kt_other, v, v_other, x, w_out_space)
    here = tok_dev // n_mem
    sent = after_space.reshape(n_grp * n_mem, here, width)
    with jax.named_scope("members_to_tokens"):
        tokens = lax.all_to_all(sent, ("grp", "mem"), split_axis=0, concat_axis=0, tiled=True)
    out = member_part(tokens, gain_member, w_qkv_member, w_out_member, gain_mlp, w_up, w_down)
    out = out.reshape(n_grp, n_mem, here, width).transpose(1, 0, 2, 3)
    with jax.named_scope("tokens_back"):
        back = lax.all_to_all(out, "mem", split_axis=0, concat_axis=0, tiled=True)
    return back.transpose(1, 0, 2, 3).reshape(mem_dev, tok_dev, width)


def solution(mesh):
    grid = Mesh(mesh.devices.reshape(8, 8, 2), ("mem", "grp", "core"))
    rows = P("mem", ("grp", "core"), None)
    return jax.shard_map(
        per_device, mesh=grid, in_specs=(rows,) + (P(),) * 9, out_specs=rows, check_vma=False
    )
```

time: 109 us -> 102 us (0.936)
  Pallas kernels: 39 us -> 31.7 us
    pallas_call x3, Pallas kernels: 19.7 us -> 15.5 us  [the longest x1 12.1 us: member_part(): pl.pallas_call(functools.partial(member_kernel, block, mlp_block, ff_step...]
    pallas_call x1, Pallas kernels: 19.3 us -> 16.2 us  [attend(): pl.pallas_call(functools.partial(attend_kernel, block, keys_step), in_spe...]
  transfers between devices with their start and end apart: 1 -> 1, of which waited for: 0 -> 1; matrix products, arithmetic and copies ran while one was open for 0% -> 0% of each run, Pallas kernels for 3% -> 2%
where the time goes in v3:
time: 102 us
  blocking collectives  67.9 us (67%)
  Pallas kernels  31.7 us (31%)
  local copies, waits for them, and re-layouts  1.2 us (1%)
    all_to_all x1, blocking collectives, per_device(): lax.all_to_all(sent, ('grp', 'mem'), split_axis=0, concat_axis=0, tiled=T...  25.3 us
    all_to_all x1, blocking collectives, per_device(): lax.all_to_all(state_field, 'grp', split_axis=0, concat_axis=0, tiled=True)  25.2 us
    all_to_all x1, blocking collectives, per_device(): back = lax.all_to_all(out, 'mem', split_axis=0, concat_axis=0, tiled=True)  17.5 us
    pallas_call x1, Pallas kernels, attend(): pl.pallas_call(functools.partial(attend_kernel, block, keys_step), in_spe...  16.2 us
    pallas_call x1, Pallas kernels, member_part(): pl.pallas_call(functools.partial(member_kernel, block, mlp_block, ff_step...  12.1 us
    pallas_call x2, Pallas kernels, project_qkv(): pl.pallas_call(functools.partial(qkv_kernel, want_q, block), in_specs=[in...  3.44 us
  transfers between devices with their start and end apart: 1, of which 1 were waited for; matrix products, arithmetic and copies ran while one was open for 0% of the time, Pallas kernels for 2%

profile of v3, /device:TPU:0, one launch (start us, length us, event | category | flops | bytes accessed | tf_op | source)
XLA Modules:
  0.0 101.5 jit_solution(17054800341327408779)
XLA Ops:
  0.0 0.0 copy-start.2
  0.0 0.0 copy-start.6
  0.0 25.2 %all_to_all.15 = bf16[8,128,512]{2,1,0:T(8,128)(2,1)S(1)} all-to-all(bf16[8,128,512]{2,1,0:T(8,128)(2,1)} %param.10), channel_id=1, replica_groups=mesh['mem'=8,'grp'=8,'core'=2] {'grp'}, dimensions={0} | all-to-all | bytes 2097152 | tf_op jit(solution)/shard_map/tokens_to_member/all_to_all | solution.py:310
  25.2 0.0 collective-permute-start
  25.2 0.0 copy-done.2
  25.2 0.0 copy-done.6
  25.2 2.1 %space_qkv.1 = (f8e4m3fn[8,1024,256]{2,1,0:T(32,128)(4,1)S(1)}, f8e4m3fn[8,256,1024]{2,1,0:T(32,128)(4,1)S(1)}, bf16[1024,512]{1,0:T(8,128)(2,1)S(1)}) custom-call(bf16[1024,512]{1,0:T(8,128)(2,1)S(1)} %bitcast.13, f32[1,512]{1,0:T(1,128)S(1)} %bitcast.17, bf16[512,1536]{1,0:T(8,128)(2,1)S(1)} %copy-done.2), custom_call_target="tpu_custom_call" | custom-call | flops 1610612736 | bytes 3145728 | tf_op jit(solution)/shard_map/space_qkv/pallas_call | solution.py:91
  27.3 0.0 copy-start.4
  27.3 0.6 collective-permute-done.x_ref
  27.9 1.4 %space_kv.1 = (f8e4m3fn[8,256,1024]{2,1,0:T(32,128)(4,1)S(1)}, bf16[1024,512]{1,0:T(8,128)(2,1)S(1)}) custom-call(bf16[1024,512]{1,0:T(8,128)(2,1)S(1)} %collective-permute-done.x_ref, f32[1,512]{1,0:T(1,128)S(1)} %bitcast.18, bf16[512,1536]{1,0:T(8,128)(2,1)S(1)} %copy-done.2), custom_call_target="tpu_custom_call" | custom-call | flops 1073741824 | bytes 3145728 | tf_op jit(solution)/shard_map/space_kv/pallas_call | solution.py:91
  29.2 0.0 copy-done.4
  29.2 0.0 copy-start.1
  29.3 0.0 copy-start.3
  29.3 0.0 copy-start.5
  29.3 16.2 %space_attend.1 = bf16[1024,512]{1,0:T(8,128)(2,1)S(1)} custom-call(f8e4m3fn[8,1024,256]{2,1,0:T(32,128)(4,1)S(1)} %get-tuple-element.10.q_ref, f8e4m3fn[8,256,1024]{2,1,0:T(32,128)(4,1)S(1)} %get-tuple-element.11.kt0, f8e4m3fn[8,256,1024]{2,1,0:T(32,128)(4,1)S(1)} %get-tuple-element.12.kt1, bf16[1024,512]{1,0:T(8,128)(2,1)S(1)} %get-tuple-element.13.v0_ref, ...), custom_call_target="tpu_custom_call" | custom-call | flops 8589934592 | bytes 12582912 | tf_op jit(solution)/shard_map/space_attend/pallas_call | solution.py:174
  45.5 0.0 copy-start
  45.5 0.0 copy-start.7
  45.5 0.0 copy-start.8
  45.5 25.3 %all_to_all.16.x_ref = bf16[64,16,512]{2,1,0:T(8,128)(2,1)S(1)} all-to-all(bf16[64,16,512]{2,1,0:T(8,128)(2,1)S(1)} %bitcast.15), channel_id=1, replica_groups=mesh['mem'=8,'grp'=8,'core'=2] {'grp','mem'}, dimensions={0} | all-to-all | bytes 2097152 | tf_op jit(solution)/shard_map/members_to_tokens/all_to_all | solution.py:320
  70.8 0.0 copy-done.1
  70.8 0.0 copy-done.3
  70.8 0.0 copy-done.5
  70.8 0.0 copy-done
  70.8 0.0 copy-done.7
  70.8 0.0 copy-done.8
  70.8 12.1 %member_part.1 = bf16[64,16,512]{2,1,0:T(8,128)(2,1)S(1)} custom-call(bf16[64,16,512]{2,1,0:T(8,128)(2,1)S(1)} %all_to_all.16.x_ref, f32[1,512]{1,0:T(1,128)S(1)} %bitcast.19, bf16[512,1536]{1,0:T(8,128)(2,1)S(1)} %copy-done.3, bf16[512,512]{1,0:T(8,128)(2,1)S(1)} %copy-done.5, f32[1,512]{1,0:T(1,128)S(1)} %bitcast.20, bf16[512,2048]{1,0:T(8,128)(2,1)S(1)} %copy-done, ...), custom_call_target="tpu_custom_call" | custom-call | flops 12884901888 | bytes 3145728 | tf_op jit(solution)/shard_map/member_part/pallas_call | solution.py:281
  82.9 0.1 copy.15
  83.0 17.5 %all_to_all.17 = bf16[8,8,16,512]{3,2,1,0:T(8,128)(2,1)S(1)} all-to-all(bf16[8,8,16,512]{3,2,1,0:T(8,128)(2,1)S(1)} %bitcast.21), channel_id=1, replica_groups=mesh['mem'=8,'grp'=8,'core'=2] {'mem'}, dimensions={0} | all-to-all | bytes 2097152 | tf_op jit(solution)/shard_map/tokens_back/all_to_all | solution.py:324
  100.5 1.1 %copy.13 = bf16[8,8,16,512]{3,2,0,1:T(8,128)(2,1)} copy(bf16[8,8,16,512]{3,2,1,0:T(8,128)(2,1)S(1)} %all_to_all.17) | data formatting | bytes 2097152 | tf_op jit(solution)/shard_map/tokens_back/all_to_all | solution.py:324
Async XLA Ops:
  0.0 25.2 %copy-start.2 = (bf16[512,1536]{1,0:T(8,128)(2,1)S(1)}, bf16[512,1536]{1,0:T(8,128)(2,1)}, u32[]{:S(2)}) copy-start(bf16[512,1536]{1,0:T(8,128)(2,1)} %w_ref.4) | copy-start | bytes 4718596
  0.0 25.2 %copy-start.6 = (f32[512]{0:T(512)S(1)}, f32[512]{0:T(512)}, u32[]{:S(2)}) copy-start(f32[512]{0:T(512)} %param.11) | copy-start | bytes 6148
  25.2 2.7 %collective-permute-start = (bf16[1024,512]{1,0:T(8,128)(2,1)S(1)}, bf16[1024,512]{1,0:T(8,128)(2,1)S(1)}, u32[]{:S(2)}, u32[]{:S(2)}) collective-permute-start(bf16[1024,512]{1,0:T(8,128)(2,1)S(1)} %bitcast.12), channel_id=1, source_target_pairs={{0,1},{1,0},{2,3},{3,2},{4,5},{5,4},{6,7},{7,6},{8,9},{9,8},{10,11... | collective-permute-start | bytes 3145736 | tf_op jit(solution)/shard_map/rows_of_other_core/ppermute | solution.py:313
  27.3 2.0 %copy-start.4 = (bf16[512,512]{1,0:T(8,128)(2,1)S(1)}, bf16[512,512]{1,0:T(8,128)(2,1)}, u32[]{:S(2)}) copy-start(bf16[512,512]{1,0:T(8,128)(2,1)} %w_ref.5) | copy-start | bytes 1572868
  29.2 41.6 %copy-start.1 = (bf16[2048,512]{1,0:T(8,128)(2,1)S(1)}, bf16[2048,512]{1,0:T(8,128)(2,1)}, u32[]{:S(2)}) copy-start(bf16[2048,512]{1,0:T(8,128)(2,1)} %wdown_ref.1) | copy-start | bytes 6291460
  29.3 41.5 %copy-start.3 = (bf16[512,1536]{1,0:T(8,128)(2,1)S(1)}, bf16[512,1536]{1,0:T(8,128)(2,1)}, u32[]{:S(2)}) copy-start(bf16[512,1536]{1,0:T(8,128)(2,1)} %wqkv_ref.1) | copy-start | bytes 4718596
  29.3 41.5 %copy-start.5 = (bf16[512,512]{1,0:T(8,128)(2,1)S(1)}, bf16[512,512]{1,0:T(8,128)(2,1)}, u32[]{:S(2)}) copy-start(bf16[512,512]{1,0:T(8,128)(2,1)} %wout_ref.1) | copy-start | bytes 1572868
  45.5 25.3 %copy-start = (bf16[512,2048]{1,0:T(8,128)(2,1)S(1)}, bf16[512,2048]{1,0:T(8,128)(2,1)}, u32[]{:S(2)}) copy-start(bf16[512,2048]{1,0:T(8,128)(2,1)} %wup_ref.1) | copy-start | bytes 6291460
  45.5 25.3 %copy-start.7 = (f32[512]{0:T(512)S(1)}, f32[512]{0:T(512)}, u32[]{:S(2)}) copy-start(f32[512]{0:T(512)} %param.14) | copy-start | bytes 6148
  45.5 25.3 %copy-start.8 = (f32[512]{0:T(512)S(1)}, f32[512]{0:T(512)}, u32[]{:S(2)}) copy-start(f32[512]{0:T(512)} %param.17) | copy-start | bytes 6148

commit v4 on v3

--- a/solution.py
+++ b/solution.py
@@ -67,15 +67,26 @@
             kt_ref[head, i * dim : (i + 1) * dim, here] = part[head * dim : (head + 1) * dim]
 
 
+def even_scales(w_ref, width):
+    tiny = 1e-06
+    both = SCORE_SCALE * (width // HEADS) ** (-0.5)
+    q_norm, k_norm = (
+        jnp.sum(jnp.square(w_ref[:, part * width : (part + 1) * width].astype(jnp.float32)), axis=0, keepdims=True)
+        for part in range(2)
+    )
+    root = jnp.sqrt(jnp.sqrt((q_norm + tiny) / (k_norm + tiny)))
+    return both**0.5 / root, both**0.5 * root
+
+
 def qkv_kernel(want_q, block, x_ref, gain_ref, w_ref, *outs):
     total, width = x_ref.shape
-    q_scale = SCORE_SCALE * 2 * (width // HEADS) ** (-0.5)
+    q_scale, k_scale = even_scales(w_ref, width)
     for b in range(total // block):
         here = slice(b * block, (b + 1) * block)
         rows = normed(x_ref[here, :].astype(jnp.float32), gain_ref[...])
         if want_q:
             put_queries(outs[0], here, dot(rows, w_ref[:, :width]) * q_scale)
-        put_keys(outs[-2], here, dot(rows, w_ref[:, width : 2 * width]) * 0.5)
+        put_keys(outs[-2], here, dot(rows, w_ref[:, width : 2 * width]) * k_scale)
         outs[-1][here, :] = dot(rows, w_ref[:, 2 * width :]).astype(jnp.bfloat16)
 
 

time: 102 us -> 102 us (level)
  no operation moved by 1% of the time
where the time goes in v4:
time: 102 us
  blocking collectives  67.9 us (67%)
  Pallas kernels  32 us (31%)
  local copies, waits for them, and re-layouts  1.2 us (1%)
    all_to_all x1, blocking collectives, per_device(): lax.all_to_all(sent, ('grp', 'mem'), split_axis=0, concat_axis=0, tiled=T...  25.2 us
    all_to_all x1, blocking collectives, per_device(): lax.all_to_all(state_field, 'grp', split_axis=0, concat_axis=0, tiled=True)  25.2 us
    all_to_all x1, blocking collectives, per_device(): back = lax.all_to_all(out, 'mem', split_axis=0, concat_axis=0, tiled=True)  17.5 us
    pallas_call x1, Pallas kernels, attend(): pl.pallas_call(functools.partial(attend_kernel, block, keys_step), in_spe...  16.2 us
    pallas_call x1, Pallas kernels, member_part(): pl.pallas_call(functools.partial(member_kernel, block, mlp_block, ff_step...  12.1 us
    pallas_call x2, Pallas kernels, project_qkv(): pl.pallas_call(functools.partial(qkv_kernel, want_q, block), in_specs=[in...  3.7 us
  transfers between devices with their start and end apart: 1, of which 1 were waited for; matrix products, arithmetic and copies ran while one was open for 0% of the time, Pallas kernels for 2%

profile of v4, /device:TPU:0, one launch (start us, length us, event | category | flops | bytes accessed | tf_op | source)
XLA Modules:
  0.0 101.6 jit_solution(3311114758028424592)
XLA Ops:
  0.0 0.0 copy-start.2
  0.0 0.0 copy-start.6
  0.0 25.2 %all_to_all.15 = bf16[8,128,512]{2,1,0:T(8,128)(2,1)S(1)} all-to-all(bf16[8,128,512]{2,1,0:T(8,128)(2,1)} %param.10), channel_id=1, replica_groups=mesh['mem'=8,'grp'=8,'core'=2] {'grp'}, dimensions={0} | all-to-all | bytes 2097152 | tf_op jit(solution)/shard_map/tokens_to_member/all_to_all | solution.py:321
  25.2 0.0 collective-permute-start
  25.2 0.0 copy-done.2
  25.2 0.0 copy-done.6
  25.2 2.2 %space_qkv.1 = (f8e4m3fn[8,1024,256]{2,1,0:T(32,128)(4,1)S(1)}, f8e4m3fn[8,256,1024]{2,1,0:T(32,128)(4,1)S(1)}, bf16[1024,512]{1,0:T(8,128)(2,1)S(1)}) custom-call(bf16[1024,512]{1,0:T(8,128)(2,1)S(1)} %bitcast.13, f32[1,512]{1,0:T(1,128)S(1)} %bitcast.17, bf16[512,1536]{1,0:T(8,128)(2,1)S(1)} %copy-done.2), custom_call_target="tpu_custom_call" | custom-call | flops 1610612736 | bytes 3145728 | tf_op jit(solution)/shard_map/space_qkv/pallas_call | solution.py:102
  27.4 0.0 copy-start.4
  27.5 0.4 collective-permute-done.x_ref
  27.9 1.5 %space_kv.1 = (f8e4m3fn[8,256,1024]{2,1,0:T(32,128)(4,1)S(1)}, bf16[1024,512]{1,0:T(8,128)(2,1)S(1)}) custom-call(bf16[1024,512]{1,0:T(8,128)(2,1)S(1)} %collective-permute-done.x_ref, f32[1,512]{1,0:T(1,128)S(1)} %bitcast.18, bf16[512,1536]{1,0:T(8,128)(2,1)S(1)} %copy-done.2), custom_call_target="tpu_custom_call" | custom-call | flops 1073741824 | bytes 3145728 | tf_op jit(solution)/shard_map/space_kv/pallas_call | solution.py:102
  29.3 0.0 copy-done.4
  29.3 0.0 copy-start.1
  29.4 0.0 copy-start.3
  29.4 0.0 copy-start.5
  29.4 16.2 %space_attend.1 = bf16[1024,512]{1,0:T(8,128)(2,1)S(1)} custom-call(f8e4m3fn[8,1024,256]{2,1,0:T(32,128)(4,1)S(1)} %get-tuple-element.10.q_ref, f8e4m3fn[8,256,1024]{2,1,0:T(32,128)(4,1)S(1)} %get-tuple-element.11.kt0, f8e4m3fn[8,256,1024]{2,1,0:T(32,128)(4,1)S(1)} %get-tuple-element.12.kt1, bf16[1024,512]{1,0:T(8,128)(2,1)S(1)} %get-tuple-element.13.v0_ref, ...), custom_call_target="tpu_custom_call" | custom-call | flops 8589934592 | bytes 12582912 | tf_op jit(solution)/shard_map/space_attend/pallas_call | solution.py:185
  45.6 0.0 copy-start
  45.6 0.0 copy-start.7
  45.6 0.0 copy-start.8
  45.6 25.2 %all_to_all.16.x_ref = bf16[64,16,512]{2,1,0:T(8,128)(2,1)S(1)} all-to-all(bf16[64,16,512]{2,1,0:T(8,128)(2,1)S(1)} %bitcast.15), channel_id=1, replica_groups=mesh['mem'=8,'grp'=8,'core'=2] {'grp','mem'}, dimensions={0} | all-to-all | bytes 2097152 | tf_op jit(solution)/shard_map/members_to_tokens/all_to_all | solution.py:331
  70.9 0.0 copy-done.1
  70.9 0.0 copy-done.3
  70.9 0.0 copy-done.5
  70.9 0.0 copy-done
  70.9 0.0 copy-done.7
  70.9 0.0 copy-done.8
  70.9 12.1 %member_part.1 = bf16[64,16,512]{2,1,0:T(8,128)(2,1)S(1)} custom-call(bf16[64,16,512]{2,1,0:T(8,128)(2,1)S(1)} %all_to_all.16.x_ref, f32[1,512]{1,0:T(1,128)S(1)} %bitcast.19, bf16[512,1536]{1,0:T(8,128)(2,1)S(1)} %copy-done.3, bf16[512,512]{1,0:T(8,128)(2,1)S(1)} %copy-done.5, f32[1,512]{1,0:T(1,128)S(1)} %bitcast.20, bf16[512,2048]{1,0:T(8,128)(2,1)S(1)} %copy-done, ...), custom_call_target="tpu_custom_call" | custom-call | flops 12884901888 | bytes 3145728 | tf_op jit(solution)/shard_map/member_part/pallas_call | solution.py:292
  83.0 0.1 copy.15
  83.1 17.5 %all_to_all.17 = bf16[8,8,16,512]{3,2,1,0:T(8,128)(2,1)S(1)} all-to-all(bf16[8,8,16,512]{3,2,1,0:T(8,128)(2,1)S(1)} %bitcast.21), channel_id=1, replica_groups=mesh['mem'=8,'grp'=8,'core'=2] {'mem'}, dimensions={0} | all-to-all | bytes 2097152 | tf_op jit(solution)/shard_map/tokens_back/all_to_all | solution.py:335
  100.6 1.1 %copy.13 = bf16[8,8,16,512]{3,2,0,1:T(8,128)(2,1)} copy(bf16[8,8,16,512]{3,2,1,0:T(8,128)(2,1)S(1)} %all_to_all.17) | data formatting | bytes 2097152 | tf_op jit(solution)/shard_map/tokens_back/all_to_all | solution.py:335
Async XLA Ops:
  0.0 25.2 %copy-start.2 = (bf16[512,1536]{1,0:T(8,128)(2,1)S(1)}, bf16[512,1536]{1,0:T(8,128)(2,1)}, u32[]{:S(2)}) copy-start(bf16[512,1536]{1,0:T(8,128)(2,1)} %w_ref.4) | copy-start | bytes 4718596
  0.0 25.2 %copy-start.6 = (f32[512]{0:T(512)S(1)}, f32[512]{0:T(512)}, u32[]{:S(2)}) copy-start(f32[512]{0:T(512)} %param.11) | copy-start | bytes 6148
  25.2 2.7 %collective-permute-start = (bf16[1024,512]{1,0:T(8,128)(2,1)S(1)}, bf16[1024,512]{1,0:T(8,128)(2,1)S(1)}, u32[]{:S(2)}, u32[]{:S(2)}) collective-permute-start(bf16[1024,512]{1,0:T(8,128)(2,1)S(1)} %bitcast.12), channel_id=1, source_target_pairs={{0,1},{1,0},{2,3},{3,2},{4,5},{5,4},{6,7},{7,6},{8,9},{9,8},{10,11... | collective-permute-start | bytes 3145736 | tf_op jit(solution)/shard_map/rows_of_other_core/ppermute | solution.py:324
  27.4 1.9 %copy-start.4 = (bf16[512,512]{1,0:T(8,128)(2,1)S(1)}, bf16[512,512]{1,0:T(8,128)(2,1)}, u32[]{:S(2)}) copy-start(bf16[512,512]{1,0:T(8,128)(2,1)} %w_ref.5) | copy-start | bytes 1572868
  29.3 41.5 %copy-start.1 = (bf16[2048,512]{1,0:T(8,128)(2,1)S(1)}, bf16[2048,512]{1,0:T(8,128)(2,1)}, u32[]{:S(2)}) copy-start(bf16[2048,512]{1,0:T(8,128)(2,1)} %wdown_ref.1) | copy-start | bytes 6291460
  29.4 41.5 %copy-start.3 = (bf16[512,1536]{1,0:T(8,128)(2,1)S(1)}, bf16[512,1536]{1,0:T(8,128)(2,1)}, u32[]{:S(2)}) copy-start(bf16[512,1536]{1,0:T(8,128)(2,1)} %wqkv_ref.1) | copy-start | bytes 4718596
  29.4 41.5 %copy-start.5 = (bf16[512,512]{1,0:T(8,128)(2,1)S(1)}, bf16[512,512]{1,0:T(8,128)(2,1)}, u32[]{:S(2)}) copy-start(bf16[512,512]{1,0:T(8,128)(2,1)} %wout_ref.1) | copy-start | bytes 1572868
  45.6 25.3 %copy-start = (bf16[512,2048]{1,0:T(8,128)(2,1)S(1)}, bf16[512,2048]{1,0:T(8,128)(2,1)}, u32[]{:S(2)}) copy-start(bf16[512,2048]{1,0:T(8,128)(2,1)} %wup_ref.1) | copy-start | bytes 6291460
  45.6 25.3 %copy-start.7 = (f32[512]{0:T(512)S(1)}, f32[512]{0:T(512)}, u32[]{:S(2)}) copy-start(f32[512]{0:T(512)} %param.14) | copy-start | bytes 6148
  45.6 25.3 %copy-start.8 = (f32[512]{0:T(512)S(1)}, f32[512]{0:T(512)}, u32[]{:S(2)}) copy-start(f32[512]{0:T(512)} %param.17) | copy-start | bytes 6148

commit v5 on v4

--- a/solution.py
+++ b/solution.py
@@ -175,10 +175,17 @@
             att[here, lanes] = jnp.where(low, done[:block], done[block:]).astype(jnp.bfloat16)
             if pair == pairs - 1:
                 out = x_ref[here, :].astype(jnp.float32) + dot(att[here, :], w_ref[...])
-                o_ref[here, :] = out.astype(jnp.bfloat16)
-
-
-def attend(q, kt0, kt1, v0, v1, x, w, block=512, keys_step=512):
+                out = out.astype(jnp.bfloat16)
+                n_xh, n_z, n_xl, n_y, tokens, _ = o_ref.shape
+                pieces = block // tokens
+                for i in range(pieces):
+                    piece = at // steps // pairs * pieces + i
+                    xh, z = divmod(piece // (n_y * n_xl), n_z)
+                    y, xl = divmod(piece % (n_y * n_xl), n_xl)
+                    o_ref[xh, z, xl, y] = out[i * tokens : (i + 1) * tokens]
+
+
+def attend(q, kt0, kt1, v0, v1, x, w, order, block=512, keys_step=512):
     rows, width = x.shape
     keys = 2 * v0.shape[0]
     in_vmem = pl.BlockSpec(memory_space=pltpu.VMEM)
@@ -186,7 +193,7 @@
         functools.partial(attend_kernel, block, keys_step),
         in_specs=[in_vmem] * 7,
         out_specs=in_vmem,
-        out_shape=jax.ShapeDtypeStruct((rows, width), jnp.bfloat16),
+        out_shape=jax.ShapeDtypeStruct(order + (rows // math.prod(order), width), jnp.bfloat16),
         scratch_shapes=[
             pltpu.VMEM((2, 2 * block, keys), jnp.float32),
             pltpu.VMEM((rows, width), jnp.bfloat16),
@@ -315,30 +322,34 @@
     w_down,
 ):
     mem_dev, tok_dev, width = state_field.shape
-    n_mem, n_grp = lax.axis_size("mem"), lax.axis_size("grp")
+    n_y, n_xl, n_z, n_xh = (lax.axis_size(name) for name in ("y", "xl", "z", "xh"))
     gain_space, gain_member, gain_mlp = (g[None] for g in (gain_space, gain_member, gain_mlp))
     with jax.named_scope("tokens_to_member"):
-        mine = lax.all_to_all(state_field, "grp", split_axis=0, concat_axis=0, tiled=True)
-    x = mine.reshape(n_grp * tok_dev, width)
+        mine = lax.all_to_all(state_field, ("xh", "z"), split_axis=0, concat_axis=0, tiled=True)
+    x = mine.reshape(n_xh * n_z * tok_dev, width)
     with jax.named_scope("rows_of_other_core"):
         x_other = lax.ppermute(x, "core", [(0, 1), (1, 0)])
     q, kt, v = project_qkv(x, gain_space, w_qkv_space, True)
     kt_other, v_other = project_qkv(x_other, gain_space, w_qkv_space, False)
-    after_space = attend(q, kt, kt_other, v, v_other, x, w_out_space)
-    here = tok_dev // n_mem
-    sent = after_space.reshape(n_grp * n_mem, here, width)
+    order = (n_xh, n_z, n_xl, n_y)
+    after_space = attend(q, kt, kt_other, v, v_other, x, w_out_space, order)
+    here = tok_dev // (n_y * n_xl)
+    sent = after_space.reshape(math.prod(order), here, width)
     with jax.named_scope("members_to_tokens"):
-        tokens = lax.all_to_all(sent, ("grp", "mem"), split_axis=0, concat_axis=0, tiled=True)
+        tokens = lax.all_to_all(
+            sent, ("xh", "z", "xl", "y"), split_axis=0, concat_axis=0, tiled=True
+        )
     out = member_part(tokens, gain_member, w_qkv_member, w_out_member, gain_mlp, w_up, w_down)
-    out = out.reshape(n_grp, n_mem, here, width).transpose(1, 0, 2, 3)
+    out = out.reshape(n_xh * n_z, n_xl * n_y, here, width).transpose(1, 0, 2, 3)
     with jax.named_scope("tokens_back"):
-        back = lax.all_to_all(out, "mem", split_axis=0, concat_axis=0, tiled=True)
-    return back.transpose(1, 0, 2, 3).reshape(mem_dev, tok_dev, width)
+        back = lax.all_to_all(out, ("xl", "y"), split_axis=0, concat_axis=0, tiled=True)
+    back = back.reshape(n_xl, n_y, n_xh, n_z, here, width).transpose(2, 3, 1, 0, 4, 5)
+    return back.reshape(mem_dev, tok_dev, width)
 
 
 def solution(mesh):
-    grid = Mesh(mesh.devices.reshape(8, 8, 2), ("mem", "grp", "core"))
-    rows = P("mem", ("grp", "core"), None)
+    grid = Mesh(mesh.devices.reshape(4, 2, 4, 2, 2), ("y", "xl", "z", "xh", "core"))
+    rows = P(("y", "xl"), ("z", "xh", "core"), None)
     return jax.shard_map(
         per_device, mesh=grid, in_specs=(rows,) + (P(),) * 9, out_specs=rows, check_vma=False
     )

time: 102 us -> 101 us (level)
    transpose x0 -> x1, local copies, waits for them, and re-layouts: none -> 1.06 us  [per_device(): back.reshape(n_xl, n_y, n_xh, n_z, here, width).transpose(2, 3, 1, 0, 4, 5)]
    all_to_all x1 -> x0, local copies, waits for them, and re-layouts: 1.06 us -> none  [per_device(): back = lax.all_to_all(out, 'mem', split_axis=0, concat_axis=0, tiled=True)]
where the time goes in v5:
time: 101 us
  blocking collectives  67.5 us (67%)
  Pallas kernels  32 us (32%)
  local copies, waits for them, and re-layouts  1.2 us (1%)
    all_to_all x1, blocking collectives, per_device(): lax.all_to_all(sent, ('xh', 'z', 'xl', 'y'), split_axis=0, concat_axis=0,...  25.4 us
    all_to_all x1, blocking collectives, per_device(): lax.all_to_all(state_field, ('xh', 'z'), split_axis=0, concat_axis=0, til...  25.1 us
    all_to_all x1, blocking collectives, per_device(): lax.all_to_all(out, ('xl', 'y'), split_axis=0, concat_axis=0, tiled=True)  17 us
    pallas_call x1, Pallas kernels, attend(): pl.pallas_call(functools.partial(attend_kernel, block, keys_step), in_spe...  16.2 us
    pallas_call x1, Pallas kernels, member_part(): pl.pallas_call(functools.partial(member_kernel, block, mlp_block, ff_step...  12.1 us
    pallas_call x2, Pallas kernels, project_qkv(): pl.pallas_call(functools.partial(qkv_kernel, want_q, block), in_specs=[in...  3.71 us
  transfers between devices with their start and end apart: 1, of which 1 were waited for; matrix products, arithmetic and copies ran while one was open for 0% of the time, Pallas kernels for 2%

profile of v5, /device:TPU:0, one launch (start us, length us, event | category | flops | bytes accessed | tf_op | source)
XLA Modules:
  0.0 101.2 jit_solution(11026035525516544393)
XLA Ops:
  0.0 0.0 copy-start.2
  0.0 0.0 copy-start.6
  0.0 25.1 %all_to_all.15 = bf16[8,128,512]{2,1,0:T(8,128)(2,1)S(1)} all-to-all(bf16[8,128,512]{2,1,0:T(8,128)(2,1)} %param.10), channel_id=1, replica_groups=mesh['y'=4,'xl'=2,'z'=4,'xh'=2,'core'=2] {'xh','z'}, dimensions={0} | all-to-all | bytes 2097152 | tf_op jit(solution)/shard_map/tokens_to_member/all_to_all | solution.py:328
  25.1 0.0 collective-permute-start
  25.1 0.0 copy-done.2
  25.1 0.0 copy-done.6
  25.1 2.2 %space_qkv.1 = (f8e4m3fn[8,1024,256]{2,1,0:T(32,128)(4,1)S(1)}, f8e4m3fn[8,256,1024]{2,1,0:T(32,128)(4,1)S(1)}, bf16[1024,512]{1,0:T(8,128)(2,1)S(1)}) custom-call(bf16[1024,512]{1,0:T(8,128)(2,1)S(1)} %bitcast.14, f32[1,512]{1,0:T(1,128)S(1)} %bitcast.18, bf16[512,1536]{1,0:T(8,128)(2,1)S(1)} %copy-done.2), custom_call_target="tpu_custom_call" | custom-call | flops 1610612736 | bytes 3145728 | tf_op jit(solution)/shard_map/space_qkv/pallas_call | solution.py:102
  27.4 0.0 copy-start.4
  27.4 0.4 collective-permute-done.x_ref
  27.8 1.5 %space_kv.1 = (f8e4m3fn[8,256,1024]{2,1,0:T(32,128)(4,1)S(1)}, bf16[1024,512]{1,0:T(8,128)(2,1)S(1)}) custom-call(bf16[1024,512]{1,0:T(8,128)(2,1)S(1)} %collective-permute-done.x_ref, f32[1,512]{1,0:T(1,128)S(1)} %bitcast.19, bf16[512,1536]{1,0:T(8,128)(2,1)S(1)} %copy-done.2), custom_call_target="tpu_custom_call" | custom-call | flops 1073741824 | bytes 3145728 | tf_op jit(solution)/shard_map/space_kv/pallas_call | solution.py:102
  29.3 0.0 copy-done.4
  29.3 0.0 copy-start.1
  29.3 0.0 copy-start.3
  29.3 0.0 copy-start.5
  29.3 16.2 %space_attend.1 = bf16[2,4,2,4,16,512]{5,4,3,2,1,0:T(8,128)(2,1)S(1)} custom-call(f8e4m3fn[8,1024,256]{2,1,0:T(32,128)(4,1)S(1)} %get-tuple-element.10.q_ref, f8e4m3fn[8,256,1024]{2,1,0:T(32,128)(4,1)S(1)} %get-tuple-element.11.kt0, f8e4m3fn[8,256,1024]{2,1,0:T(32,128)(4,1)S(1)} %get-tuple-element.12.kt1, bf16[1024,512]{1,0:T(8,128)(2,1)S(1)} %get-tuple-element.13.v0_ref, ...), custom_call_target="tpu_custom_call" | custom-call | flops 8589934592 | bytes 12582912 | tf_op jit(solution)/shard_map/space_attend/pallas_call | solution.py:192
  45.5 0.0 copy-start
  45.6 0.0 copy-start.7
  45.6 0.0 copy-start.8
  45.6 25.4 %all_to_all.16.x_ref = bf16[64,16,512]{2,1,0:T(8,128)(2,1)S(1)} all-to-all(bf16[64,16,512]{2,1,0:T(8,128)(2,1)S(1)} %bitcast.16), channel_id=1, replica_groups=mesh['y'=4,'xl'=2,'z'=4,'xh'=2,'core'=2] {'xh','z','xl','y'}, dimensions={0} | all-to-all | bytes 2097152 | tf_op jit(solution)/shard_map/members_to_tokens/all_to_all | solution.py:339
  71.0 0.0 copy-done.1
  71.0 0.0 copy-done.3
  71.0 0.0 copy-done.5
  71.0 0.0 copy-done
  71.0 0.0 copy-done.7
  71.0 0.0 copy-done.8
  71.0 12.1 %member_part.1 = bf16[64,16,512]{2,1,0:T(8,128)(2,1)S(1)} custom-call(bf16[64,16,512]{2,1,0:T(8,128)(2,1)S(1)} %all_to_all.16.x_ref, f32[1,512]{1,0:T(1,128)S(1)} %bitcast.20, bf16[512,1536]{1,0:T(8,128)(2,1)S(1)} %copy-done.3, bf16[512,512]{1,0:T(8,128)(2,1)S(1)} %copy-done.5, f32[1,512]{1,0:T(1,128)S(1)} %bitcast.21, bf16[512,2048]{1,0:T(8,128)(2,1)S(1)} %copy-done, ...), custom_call_target="tpu_custom_call" | custom-call | flops 12884901888 | bytes 3145728 | tf_op jit(solution)/shard_map/member_part/pallas_call | solution.py:299
  83.1 0.1 copy.15
  83.2 17.0 %all_to_all.17 = bf16[8,8,16,512]{3,2,1,0:T(8,128)(2,1)S(1)} all-to-all(bf16[8,8,16,512]{3,2,1,0:T(8,128)(2,1)S(1)} %bitcast.22), channel_id=1, replica_groups=mesh['y'=4,'xl'=2,'z'=4,'xh'=2,'core'=2] {'xl','y'}, dimensions={0} | all-to-all | bytes 2097152 | tf_op jit(solution)/shard_map/tokens_back/all_to_all | solution.py:345
  100.2 1.1 %copy.13 = bf16[2,4,4,2,16,512]{5,4,3,2,1,0:T(8,128)(2,1)} copy(bf16[2,4,4,2,16,512]{5,4,1,0,2,3:T(8,128)(2,1)S(1)} %bitcast.23) | data formatting | bytes 2097152 | tf_op jit(solution)/shard_map/transpose | solution.py:346
Async XLA Ops:
  0.0 25.1 %copy-start.2 = (bf16[512,1536]{1,0:T(8,128)(2,1)S(1)}, bf16[512,1536]{1,0:T(8,128)(2,1)}, u32[]{:S(2)}) copy-start(bf16[512,1536]{1,0:T(8,128)(2,1)} %w_ref.4) | copy-start | bytes 4718596
  0.0 25.1 %copy-start.6 = (f32[512]{0:T(512)S(1)}, f32[512]{0:T(512)}, u32[]{:S(2)}) copy-start(f32[512]{0:T(512)} %param.11) | copy-start | bytes 6148
  25.1 2.7 %collective-permute-start = (bf16[1024,512]{1,0:T(8,128)(2,1)S(1)}, bf16[1024,512]{1,0:T(8,128)(2,1)S(1)}, u32[]{:S(2)}, u32[]{:S(2)}) collective-permute-start(bf16[1024,512]{1,0:T(8,128)(2,1)S(1)} %bitcast.13), channel_id=1, source_target_pairs={{0,1},{1,0},{2,3},{3,2},{4,5},{5,4},{6,7},{7,6},{8,9},{9,8},{10,11... | collective-permute-start | bytes 3145736 | tf_op jit(solution)/shard_map/rows_of_other_core/ppermute | solution.py:331
  27.4 1.9 %copy-start.4 = (bf16[512,512]{1,0:T(8,128)(2,1)S(1)}, bf16[512,512]{1,0:T(8,128)(2,1)}, u32[]{:S(2)}) copy-start(bf16[512,512]{1,0:T(8,128)(2,1)} %w_ref.5) | copy-start | bytes 1572868
  29.3 41.7 %copy-start.1 = (bf16[2048,512]{1,0:T(8,128)(2,1)S(1)}, bf16[2048,512]{1,0:T(8,128)(2,1)}, u32[]{:S(2)}) copy-start(bf16[2048,512]{1,0:T(8,128)(2,1)} %wdown_ref.1) | copy-start | bytes 6291460
  29.3 41.7 %copy-start.3 = (bf16[512,1536]{1,0:T(8,128)(2,1)S(1)}, bf16[512,1536]{1,0:T(8,128)(2,1)}, u32[]{:S(2)}) copy-start(bf16[512,1536]{1,0:T(8,128)(2,1)} %wqkv_ref.1) | copy-start | bytes 4718596
  29.3 41.7 %copy-start.5 = (bf16[512,512]{1,0:T(8,128)(2,1)S(1)}, bf16[512,512]{1,0:T(8,128)(2,1)}, u32[]{:S(2)}) copy-start(bf16[512,512]{1,0:T(8,128)(2,1)} %wout_ref.1) | copy-start | bytes 1572868
  45.5 25.4 %copy-start = (bf16[512,2048]{1,0:T(8,128)(2,1)S(1)}, bf16[512,2048]{1,0:T(8,128)(2,1)}, u32[]{:S(2)}) copy-start(bf16[512,2048]{1,0:T(8,128)(2,1)} %wup_ref.1) | copy-start | bytes 6291460
  45.6 25.4 %copy-start.7 = (f32[512]{0:T(512)S(1)}, f32[512]{0:T(512)}, u32[]{:S(2)}) copy-start(f32[512]{0:T(512)} %param.14) | copy-start | bytes 6148
  45.6 25.4 %copy-start.8 = (f32[512]{0:T(512)S(1)}, f32[512]{0:T(512)}, u32[]{:S(2)}) copy-start(f32[512]{0:T(512)} %param.17) | copy-start | bytes 6148

commit v6 on v5

--- a/solution.py
+++ b/solution.py
@@ -26,6 +26,12 @@
 def normed(values, gain):
     scaled = values * lax.rsqrt(jnp.mean(values * values, axis=-1, keepdims=True) + 1e-05)
     return (scaled * gain).astype(jnp.bfloat16)
+
+
+def gelu(x):
+    c = (2 / math.pi) ** 0.5
+    half = 0.5 * x
+    return half + half * jnp.tanh(x * (c + (c * 0.044715) * (x * x)))
 
 
 def dot(a, b):
@@ -277,7 +283,7 @@
         up = dot(n, wup_ref[:, :ff_step])
         for j in range(0, ff, ff_step):
             later = dot(n, wup_ref[:, j + ff_step : j + 2 * ff_step]) if j + ff_step < ff else None
-            hidden = jax.nn.gelu(up, approximate=True).astype(jnp.bfloat16)
+            hidden = gelu(up).astype(jnp.bfloat16)
             out = out + dot(hidden, wdown_ref[j : j + ff_step, :])
             up = later
         for t in range(mlp_block // members):
@@ -292,7 +298,7 @@
         )
 
 
-def member_part(x, gain, wqkv, wout, gain2, wup, wdown, block=256, mlp_block=512, ff_step=256):
+def member_part(x, gain, wqkv, wout, gain2, wup, wdown, block=256, mlp_block=1024, ff_step=256):
     members, tokens, width = x.shape
     total, ff = members * tokens, wup.shape[1]
     in_vmem = pl.BlockSpec(memory_space=pltpu.VMEM)
@@ -303,7 +309,7 @@
         out_shape=jax.ShapeDtypeStruct((members, tokens, width), jnp.bfloat16),
         scratch_shapes=[pltpu.VMEM((width // LANES, total, LANES), jnp.float32)]
         + [pltpu.VMEM((total, width), jnp.bfloat16)] * 4,
-        compiler_params=params(24),
+        compiler_params=params(32),
         cost_estimate=cost(total * width * 2 * (4 * width + 2 * ff) * 2, 6 * total * width),
         name="member_part",
     )(x, gain, wqkv, wout, gain2, wup, wdown)

time: 101 us -> 101 us (level)
  no operation moved by 1% of the time
where the time goes in v6:
time: 101 us
  blocking collectives  67.5 us (67%)
  Pallas kernels  31.6 us (31%)
  local copies, waits for them, and re-layouts  1.2 us (1%)
    all_to_all x1, blocking collectives, per_device(): lax.all_to_all(sent, ('xh', 'z', 'xl', 'y'), split_axis=0, concat_axis=0,...  25.4 us
    all_to_all x1, blocking collectives, per_device(): lax.all_to_all(state_field, ('xh', 'z'), split_axis=0, concat_axis=0, til...  25.1 us
    all_to_all x1, blocking collectives, per_device(): lax.all_to_all(out, ('xl', 'y'), split_axis=0, concat_axis=0, tiled=True)  17 us
    pallas_call x1, Pallas kernels, attend(): pl.pallas_call(functools.partial(attend_kernel, block, keys_step), in_spe...  16.2 us
    pallas_call x1, Pallas kernels, member_part(): pl.pallas_call(functools.partial(member_kernel, block, mlp_block, ff_step...  11.7 us
    pallas_call x2, Pallas kernels, project_qkv(): pl.pallas_call(functools.partial(qkv_kernel, want_q, block), in_specs=[in...  3.71 us
  transfers between devices with their start and end apart: 1, of which 1 were waited for; matrix products, arithmetic and copies ran while one was open for 0% of the time, Pallas kernels for 2%

profile of v6, /device:TPU:0, one launch (start us, length us, event | category | flops | bytes accessed | tf_op | source)
XLA Modules:
  0.0 100.8 jit_solution(7020468261822655336)
XLA Ops:
  0.0 0.0 copy-start.2
  0.0 0.0 copy-start.6
  0.0 25.1 %all_to_all.15 = bf16[8,128,512]{2,1,0:T(8,128)(2,1)S(1)} all-to-all(bf16[8,128,512]{2,1,0:T(8,128)(2,1)} %param.10), channel_id=1, replica_groups=mesh['y'=4,'xl'=2,'z'=4,'xh'=2,'core'=2] {'xh','z'}, dimensions={0} | all-to-all | bytes 2097152 | tf_op jit(solution)/shard_map/tokens_to_member/all_to_all | solution.py:334
  25.1 0.0 collective-permute-start
  25.1 0.0 copy-done.2
  25.1 0.0 copy-done.6
  25.1 2.2 %space_qkv.1 = (f8e4m3fn[8,1024,256]{2,1,0:T(32,128)(4,1)S(1)}, f8e4m3fn[8,256,1024]{2,1,0:T(32,128)(4,1)S(1)}, bf16[1024,512]{1,0:T(8,128)(2,1)S(1)}) custom-call(bf16[1024,512]{1,0:T(8,128)(2,1)S(1)} %bitcast.14, f32[1,512]{1,0:T(1,128)S(1)} %bitcast.18, bf16[512,1536]{1,0:T(8,128)(2,1)S(1)} %copy-done.2), custom_call_target="tpu_custom_call" | custom-call | flops 1610612736 | bytes 3145728 | tf_op jit(solution)/shard_map/space_qkv/pallas_call | solution.py:108
  27.4 0.0 copy-start.4
  27.4 0.4 collective-permute-done.x_ref
  27.8 1.5 %space_kv.1 = (f8e4m3fn[8,256,1024]{2,1,0:T(32,128)(4,1)S(1)}, bf16[1024,512]{1,0:T(8,128)(2,1)S(1)}) custom-call(bf16[1024,512]{1,0:T(8,128)(2,1)S(1)} %collective-permute-done.x_ref, f32[1,512]{1,0:T(1,128)S(1)} %bitcast.19, bf16[512,1536]{1,0:T(8,128)(2,1)S(1)} %copy-done.2), custom_call_target="tpu_custom_call" | custom-call | flops 1073741824 | bytes 3145728 | tf_op jit(solution)/shard_map/space_kv/pallas_call | solution.py:108
  29.3 0.0 copy-done.4
  29.3 0.0 copy-start.1
  29.3 0.0 copy-start.3
  29.3 0.0 copy-start.5
  29.3 16.2 %space_attend.1 = bf16[2,4,2,4,16,512]{5,4,3,2,1,0:T(8,128)(2,1)S(1)} custom-call(f8e4m3fn[8,1024,256]{2,1,0:T(32,128)(4,1)S(1)} %get-tuple-element.10.q_ref, f8e4m3fn[8,256,1024]{2,1,0:T(32,128)(4,1)S(1)} %get-tuple-element.11.kt0, f8e4m3fn[8,256,1024]{2,1,0:T(32,128)(4,1)S(1)} %get-tuple-element.12.kt1, bf16[1024,512]{1,0:T(8,128)(2,1)S(1)} %get-tuple-element.13.v0_ref, ...), custom_call_target="tpu_custom_call" | custom-call | flops 8589934592 | bytes 12582912 | tf_op jit(solution)/shard_map/space_attend/pallas_call | solution.py:198
  45.5 0.0 copy-start
  45.6 0.0 copy-start.7
  45.6 0.0 copy-start.8
  45.6 25.4 %all_to_all.16.x_ref = bf16[64,16,512]{2,1,0:T(8,128)(2,1)S(1)} all-to-all(bf16[64,16,512]{2,1,0:T(8,128)(2,1)S(1)} %bitcast.16), channel_id=1, replica_groups=mesh['y'=4,'xl'=2,'z'=4,'xh'=2,'core'=2] {'xh','z','xl','y'}, dimensions={0} | all-to-all | bytes 2097152 | tf_op jit(solution)/shard_map/members_to_tokens/all_to_all | solution.py:345
  71.0 0.0 copy-done.1
  71.0 0.0 copy-done.3
  71.0 0.0 copy-done.5
  71.0 0.0 copy-done
  71.0 0.0 copy-done.7
  71.0 0.0 copy-done.8
  71.0 11.7 %member_part.1 = bf16[64,16,512]{2,1,0:T(8,128)(2,1)S(1)} custom-call(bf16[64,16,512]{2,1,0:T(8,128)(2,1)S(1)} %all_to_all.16.x_ref, f32[1,512]{1,0:T(1,128)S(1)} %bitcast.20, bf16[512,1536]{1,0:T(8,128)(2,1)S(1)} %copy-done.3, bf16[512,512]{1,0:T(8,128)(2,1)S(1)} %copy-done.5, f32[1,512]{1,0:T(1,128)S(1)} %bitcast.21, bf16[512,2048]{1,0:T(8,128)(2,1)S(1)} %copy-done, ...), custom_call_target="tpu_custom_call" | custom-call | flops 12884901888 | bytes 3145728 | tf_op jit(solution)/shard_map/member_part/pallas_call | solution.py:305
  82.7 0.1 copy.15
  82.8 17.0 %all_to_all.17 = bf16[8,8,16,512]{3,2,1,0:T(8,128)(2,1)S(1)} all-to-all(bf16[8,8,16,512]{3,2,1,0:T(8,128)(2,1)S(1)} %bitcast.22), channel_id=1, replica_groups=mesh['y'=4,'xl'=2,'z'=4,'xh'=2,'core'=2] {'xl','y'}, dimensions={0} | all-to-all | bytes 2097152 | tf_op jit(solution)/shard_map/tokens_back/all_to_all | solution.py:351
  99.8 1.1 %copy.13 = bf16[2,4,4,2,16,512]{5,4,3,2,1,0:T(8,128)(2,1)} copy(bf16[2,4,4,2,16,512]{5,4,1,0,2,3:T(8,128)(2,1)S(1)} %bitcast.23) | data formatting | bytes 2097152 | tf_op jit(solution)/shard_map/transpose | solution.py:352
Async XLA Ops:
  0.0 25.1 %copy-start.2 = (bf16[512,1536]{1,0:T(8,128)(2,1)S(1)}, bf16[512,1536]{1,0:T(8,128)(2,1)}, u32[]{:S(2)}) copy-start(bf16[512,1536]{1,0:T(8,128)(2,1)} %w_ref.4) | copy-start | bytes 4718596
  0.0 25.1 %copy-start.6 = (f32[512]{0:T(512)S(1)}, f32[512]{0:T(512)}, u32[]{:S(2)}) copy-start(f32[512]{0:T(512)} %param.11) | copy-start | bytes 6148
  25.1 2.7 %collective-permute-start = (bf16[1024,512]{1,0:T(8,128)(2,1)S(1)}, bf16[1024,512]{1,0:T(8,128)(2,1)S(1)}, u32[]{:S(2)}, u32[]{:S(2)}) collective-permute-start(bf16[1024,512]{1,0:T(8,128)(2,1)S(1)} %bitcast.13), channel_id=1, source_target_pairs={{0,1},{1,0},{2,3},{3,2},{4,5},{5,4},{6,7},{7,6},{8,9},{9,8},{10,11... | collective-permute-start | bytes 3145736 | tf_op jit(solution)/shard_map/rows_of_other_core/ppermute | solution.py:337
  27.4 1.9 %copy-start.4 = (bf16[512,512]{1,0:T(8,128)(2,1)S(1)}, bf16[512,512]{1,0:T(8,128)(2,1)}, u32[]{:S(2)}) copy-start(bf16[512,512]{1,0:T(8,128)(2,1)} %w_ref.5) | copy-start | bytes 1572868
  29.3 41.7 %copy-start.1 = (bf16[2048,512]{1,0:T(8,128)(2,1)S(1)}, bf16[2048,512]{1,0:T(8,128)(2,1)}, u32[]{:S(2)}) copy-start(bf16[2048,512]{1,0:T(8,128)(2,1)} %wdown_ref.1) | copy-start | bytes 6291460
  29.3 41.7 %copy-start.3 = (bf16[512,1536]{1,0:T(8,128)(2,1)S(1)}, bf16[512,1536]{1,0:T(8,128)(2,1)}, u32[]{:S(2)}) copy-start(bf16[512,1536]{1,0:T(8,128)(2,1)} %wqkv_ref.1) | copy-start | bytes 4718596
  29.3 41.7 %copy-start.5 = (bf16[512,512]{1,0:T(8,128)(2,1)S(1)}, bf16[512,512]{1,0:T(8,128)(2,1)}, u32[]{:S(2)}) copy-start(bf16[512,512]{1,0:T(8,128)(2,1)} %wout_ref.1) | copy-start | bytes 1572868
  45.5 25.4 %copy-start = (bf16[512,2048]{1,0:T(8,128)(2,1)S(1)}, bf16[512,2048]{1,0:T(8,128)(2,1)}, u32[]{:S(2)}) copy-start(bf16[512,2048]{1,0:T(8,128)(2,1)} %wup_ref.1) | copy-start | bytes 6291460
  45.6 25.4 %copy-start.7 = (f32[512]{0:T(512)S(1)}, f32[512]{0:T(512)}, u32[]{:S(2)}) copy-start(f32[512]{0:T(512)} %param.14) | copy-start | bytes 6148
  45.6 25.4 %copy-start.8 = (f32[512]{0:T(512)S(1)}, f32[512]{0:T(512)}, u32[]{:S(2)}) copy-start(f32[512]{0:T(512)} %param.17) | copy-start | bytes 6148
